TPU v7x, 512 devices: a whole 4x4x16 slice. The times are simulated.
512 devices in a mesh: facet: 16 (over z), col: 32 (over x, y, core).
Axes of the slice: x: 4, y: 4, z: 16, core: 2. Of those that a mesh axis runs over, the one named last changes fastest.
Arguments:
- sky_re: bfloat16 [16, 4096, 4096], P('facet', None, 'col'), may hold values from -6 to 6
- sky_im: bfloat16 [16, 4096, 4096], P('facet', None, 'col'), may hold values from -6 to 6
- col_offsets: int32 [2], replicated, may hold values from 0 to 65280
- sub_offsets: int32 [16], replicated, may hold values from 0 to 65280
- kernel: float32 [16, 8], replicated, may hold values from 0.05 to 1
- vis_count: int32 [16, 128], P('facet', 'col'), may hold values from 0 to 128, as said below
- cell_index: int32 [2, 16, 128, 128], P(None, 'facet', 'col'), may hold values from 0 to 248
- frac_index: int32 [2, 16, 128, 128], P(None, 'facet', 'col'), may hold values from 0 to 15
Outputs:
- vis_re: float32 [16, 128, 128], P('facet', 'col')
- vis_im: float32 [16, 128, 128], P('facet', 'col')
Inputs may be any that keep to these rules, and one draw needn't show every extreme that they name: Within each subgrid the blocks with visibilities come first and block 0 holds 128; in some subgrid all 128 blocks hold visibilities; a block's visibilities fill its first vis_count slots.
All inputs are finite; a program needn't handle non-finite values.
Results may differ from a plain program's by a relative error of at most 0.0037.
Values may be sent and summed in bfloat16 or wider, within the bound.
No kernel may reach another device: no remote copies, remote signals or barrier semaphores. Data moves between devices by JAX's collectives and lax.ppermute only.
A program may use at most 64 MiB of HBM per device.

v0:
```python
import math

import jax
import jax.numpy as jnp
from jax import lax
from jax.sharding import PartitionSpec as P

N_IMG = 65536
S = 256
SCOL = 2


def in_blocks(x, dim, peers):
    before, after = (x.shape[:dim], x.shape[dim + 1 :])
    return jnp.moveaxis(x.reshape(*before, peers, -1, *after), dim, 0)


def summed_on_arrival(x, axis, dim):
    pieces = in_blocks(x, dim, lax.axis_size(axis))
    arrived = lax.all_to_all(pieces, axis, split_axis=0, concat_axis=0, tiled=True)
    return arrived.sum(axis=0)


def in_order(pieces, dim):
    dims = list(pieces.shape[1:])
    dims[dim] *= pieces.shape[0]
    return jnp.moveaxis(pieces, 0, dim).reshape(dims)


def copy_for_each(x, axis):
    copies = jnp.broadcast_to(x, (lax.axis_size(axis), *x.shape))
    return lax.all_to_all(copies, axis, split_axis=0, concat_axis=0, tiled=True)


def collect(x, axis, dim):
    return in_order(copy_for_each(x, axis), dim)


def modular_product(left_ints, right_ints):
    upper_part = right_ints // 256
    lower_part = right_ints % 256
    product = left_ints[:, None] * upper_part[None, :] % N_IMG
    product = product * 256 % N_IMG
    return (product + left_ints[:, None] * lower_part[None, :]) % N_IMG


def cos_sin(left_ints, right_ints, factor):
    angles = modular_product(left_ints, right_ints).astype(jnp.float32) * (2.0 * math.pi / N_IMG)
    return (jnp.cos(angles) * factor, jnp.sin(angles) * factor)


def first_axis(facet_image, table, local_cols):
    product = jnp.dot(table, facet_image, preferred_element_type=jnp.float32)
    real_part = product[:S, :local_cols] + product[S:, local_cols:]
    imag_part = product[:S, local_cols:] - product[S:, :local_cols]
    return jnp.stack([real_part, imag_part]).astype(jnp.bfloat16)


def second_axis(band_rows, starts, anchor, second_table):
    mod_cos, mod_sin = cos_sin(starts, anchor, 1.0)
    shifted_re = band_rows[0][None] * mod_cos[:, None] + band_rows[1][None] * mod_sin[:, None]
    shifted_im = band_rows[1][None] * mod_cos[:, None] - band_rows[0][None] * mod_sin[:, None]
    stacked = jnp.concatenate([shifted_re, shifted_im], axis=0).astype(jnp.bfloat16)
    per_column = starts.shape[0]
    row_count = band_rows.shape[1]
    product = jnp.dot(
        stacked.reshape(2 * per_column * row_count, -1),
        second_table,
        preferred_element_type=jnp.float32,
    )
    product = product.reshape(2, per_column, row_count, 2 * S)
    term_re = product[0, :, :, :S] + product[1, :, :, S:]
    term_im = product[1, :, :, :S] - product[0, :, :, S:]
    return jnp.concatenate([term_re, term_im], axis=2)


def lookup(frac_ints, kernel):
    table_rows = jnp.arange(kernel.shape[0], dtype=jnp.int32)
    matches = frac_ints[..., None] == table_rows
    return jnp.sum(jnp.where(matches[..., None], kernel, 0.0), axis=-2)


def spread(cell_ints, tap_values):
    columns = jnp.arange(S, dtype=jnp.int32)
    summed = jnp.zeros(cell_ints.shape + (S,), jnp.float32)
    for offset in range(tap_values.shape[-1]):
        summed = summed + jnp.where(
            columns == cell_ints[..., None] + offset, tap_values[..., offset : offset + 1], 0.0
        )
    return summed


def visibilities(row_sum, col_weights, in_block):
    vis_real = jnp.where(in_block, jnp.sum(row_sum[..., :S] * col_weights, axis=-1), 0.0)
    vis_imag = jnp.where(in_block, jnp.sum(row_sum[..., S:] * col_weights, axis=-1), 0.0)
    return (vis_real, vis_imag)


def facet_table(facet_anchor, spectral, pixels, facets):
    cos_tab, sin_tab = cos_sin(facet_anchor, spectral, 1.0 / math.sqrt(pixels * facets))
    return jnp.concatenate([cos_tab, sin_tab], axis=1).astype(jnp.bfloat16)


def local(sky_re, sky_im, col_offsets, sub_offsets, kernel, vis_count, cell_index, frac_index):
    pixels = sky_re.shape[1]
    local_cols = sky_re.shape[2]
    facets = lax.axis_size("facet")
    per_column = sub_offsets.shape[0] // SCOL
    owned = vis_count.shape[0]
    facet_image = jnp.concatenate([sky_re[0], sky_im[0]], axis=1)
    spatial = jnp.arange(pixels, dtype=jnp.int32)
    spectral = jnp.arange(S, dtype=jnp.int32)

    def column_table(column):
        cos_part, sin_part = cos_sin(
            col_offsets[column] + spectral, spatial, 1.0 / math.sqrt(pixels)
        )
        return jnp.concatenate([cos_part, sin_part], axis=0).astype(jnp.bfloat16)

    def column_starts(column):
        return sub_offsets[column * per_column : (column + 1) * per_column]

    pieces = jnp.stack(
        [first_axis(facet_image, column_table(column), local_cols) for column in range(SCOL)]
    )
    received = lax.all_to_all(pieces, "col", split_axis=2, concat_axis=3, tiled=True)
    column_bands = [received[column] for column in range(SCOL)]
    anchor = lax.axis_index("facet") * pixels + spatial
    second_table = facet_table(anchor, spectral, pixels, facets)
    column_terms = [
        second_axis(column_bands[column], column_starts(column), anchor, second_table)
        for column in range(SCOL)
    ]
    partial_value = jnp.concatenate(column_terms, axis=0)
    grid_rows = summed_on_arrival(partial_value, "facet", 0).astype(jnp.bfloat16)
    blocks = vis_count.shape[1]
    block_slots = cell_index.shape[-1]
    slot_ids = jnp.arange(block_slots, dtype=jnp.int32)
    row_weights = spread(cell_index[0], lookup(frac_index[0], kernel)).astype(jnp.bfloat16)
    row_weights = row_weights.reshape(owned, blocks * block_slots, S)
    col_weights = spread(cell_index[1], lookup(frac_index[1], kernel)).reshape(
        owned, blocks * block_slots, S
    )
    row_sum = jnp.einsum(
        "svr,src->svc",
        row_weights,
        collect(grid_rows, "col", 1),
        preferred_element_type=jnp.float32,
    )
    in_block = (slot_ids < vis_count[..., None]).reshape(owned, blocks * block_slots)
    flat_re, flat_im = visibilities(row_sum, col_weights, in_block)
    vis_real = flat_re.reshape(owned, blocks, block_slots)
    vis_imag = flat_im.reshape(owned, blocks, block_slots)
    return (vis_real, vis_imag)


def solution(mesh):
    placed = (
        P("facet", None, "col"),
        P("facet", None, "col"),
        P(),
        P(),
        P(),
        P("facet", "col"),
        P(None, "facet", "col", None),
        P(None, "facet", "col", None),
    )
    return jax.shard_map(
        local,
        mesh=mesh,
        in_specs=placed,
        out_specs=(P("facet", "col", None), P("facet", "col", None)),
        check_vma=False,
    )
```

profile of v0, /device:TPU:1, one launch (start us, length us, event | category | flops | bytes accessed | tf_op | source)
XLA Modules:
  0.0 139.2 jit_solution(3544712988015101752)
XLA Ops:
  0.6 1.3 fusion.103
  2.0 1.3 iota_add_fusion.1
  3.3 40.9 %multiply_convert_fusion.5 = (bf16[256,4096]{1,0:T(8,128)(2,1)S(1)}, bf16[256,4096]{1,0:T(8,128)(2,1)S(1)}, bf16[256,4096]{1,0:T(8,128)(2,1)S(1)}, bf16[256,4096]{1,0:T(8,128)(2,1)S(1)}) fusion(s32[4096]{0:T(1024)S(1)} %get-tuple-element.78, s32[4096]{0:T(1024)S(1)} %get-tuple-element.79, s32[256]{0:T(256)S(1)} %get-tuple-element.81, ...), kind=kLoop, calls=%fused_computation.68 | loop fusion | flops 90177536 | bytes 8423424 | tf_op jit(solution)/shard_map/convert.20
  44.2 1.2 fusion.21
  45.5 1.2 fusion.25
  46.8 1.0 copy.16
  47.8 10.4 %all-to-all-start = ((bf16[2,2,256,128]{3,1,0,2:T(2,128)(2,1)}), bf16[2,2,256,128]{3,1,0,2:T(2,128)(2,1)S(1)}, u32[]{:S(2)}, u32[]{:S(2)}) async-start(bf16[2,2,256,128]{3,1,0,2:T(2,128)(2,1)} %copy.16), calls=%async_computation | async-start | bytes 524288 | tf_op jit(solution)/shard_map/all_to_all | solution.py:126
  58.3 22.9 %multiply_convert_fusion.1 = (bf16[4096,256]{1,0:T(8,128)(2,1)S(1)}, bf16[4096,256]{1,0:T(8,128)(2,1)}) fusion(s32[256]{0:T(256)S(1)} %get-tuple-element.82, s32[256]{0:T(256)S(1)} %get-tuple-element.83, s32[4096]{0:T(1024)S(1)} %iota_add_fusion), kind=kLoop, calls=%fused_computation.64 | loop fusion | flops 45088768 | bytes 4212736 | tf_op jit(solution)/shard_map/convert.6
  81.2 1.3 fusion.80
  82.6 0.4 slice_convert_fusion.3
  83.0 0.2 add_convert_fusion.1
  83.3 1.2 copy-done
  84.6 0.7 fusion.30
  85.3 0.2 add_convert_fusion
  85.7 0.7 fusion.29
  86.4 0.7 maximum_bitcast_fusion.3
  87.2 13.1 %all-to-all-start.1 = ((f32[16,1,8,512]{3,2,1,0:T(8,128)}), f32[16,1,8,512]{3,2,1,0:T(8,128)S(1)}, u32[]{:S(2)}, u32[]{:S(2)}) async-start(f32[16,1,8,512]{3,2,1,0:T(8,128)} %maximum_bitcast_fusion.3), calls=%async_computation.1 | async-start | bytes 524288 | tf_op jit(solution)/shard_map/all_to_all | solution.py:20
  100.5 13.9 %all-to-all-done.1 = f32[16,1,8,512]{3,2,1,0:T(8,128)S(1)} async-done(((f32[16,1,8,512]{3,2,1,0:T(8,128)}), f32[16,1,8,512]{3,2,1,0:T(8,128)S(1)}, u32[]{:S(2)}, u32[]{:S(2)}) %all-to-all-start.1) | async-done | bytes 262176 | tf_op jit(solution)/shard_map/all_to_all | solution.py:20
  114.4 0.7 broadcast_in_dim.237
  115.2 12.1 %all-to-all-start.2 = ((bf16[32,1,8,512]{3,2,1,0:T(8,128)(2,1)}), bf16[32,1,8,512]{3,2,1,0:T(8,128)(2,1)S(1)}, u32[]{:S(2)}, u32[]{:S(2)}) async-start(bf16[32,1,8,512]{3,2,1,0:T(8,128)(2,1)} %broadcast_in_dim.237), calls=%async_computation.2 | async-start | bytes 524288 | tf_op jit(solution)/shard_map/all_to_all | solution.py:32
  127.3 9.0 %all-to-all-done.2 = bf16[32,1,8,512]{3,2,1,0:T(8,128)(2,1)S(1)} async-done(((bf16[32,1,8,512]{3,2,1,0:T(8,128)(2,1)}), bf16[32,1,8,512]{3,2,1,0:T(8,128)(2,1)S(1)}, u32[]{:S(2)}, u32[]{:S(2)}) %all-to-all-start.2) | async-done | bytes 262176 | tf_op jit(solution)/shard_map/all_to_all | solution.py:32
  136.3 1.8 %convolution_bitcast_fusion = f32[1,512,512]{1,2,0:T(8,128)S(1)} fusion(bf16[32,1,8,512]{3,2,1,0:T(8,128)(2,1)S(1)} %all-to-all-done.2, f32[512]{0:T(512)S(1)} %bitcast.123, s32[512]{0:T(512)S(1)} %get-tuple-element.67, f32[512]{0:T(512)S(1)} %bitcast.124, s32[512]{0:T(512)S(1)} %get-tuple-element.66, f32[512]{0:T(512)S(1)} %bitcast.125, ...), kind=kOutput, calls=%fused_computation.72 | convolution fusion | flops 137363456 | bytes 1343488 | tf_op jit(solution)/shard_map/svr,src->svc/dot_general | solution.py:144
  138.1 0.5 fusion.31
  138.6 0.7 bitcast_select_fusion
  (37 shorter events, 0.7 us)
Async XLA Ops:
  3.3 40.9 %copy-start.6 = (bf16[1,4096,128]{2,1,0:T(8,128)(2,1)S(1)}, bf16[1,4096,128]{2,1,0:T(8,128)(2,1)}, u32[]{:S(2)}) copy-start(bf16[1,4096,128]{2,1,0:T(8,128)(2,1)} %param.9) | copy-start | bytes 3145732
  3.3 40.9 %copy-start.7 = (bf16[1,4096,128]{2,1,0:T(8,128)(2,1)S(1)}, bf16[1,4096,128]{2,1,0:T(8,128)(2,1)}, u32[]{:S(2)}) copy-start(bf16[1,4096,128]{2,1,0:T(8,128)(2,1)} %param.8) | copy-start | bytes 3145732
  46.7 11.5 %copy-start.4 = (s32[16]{0:T(128)S(1)}, s32[16]{0:T(128)}, u32[]{:S(2)}) copy-start(s32[16]{0:T(128)} %param.11) | copy-start | bytes 196
  47.8 34.8 %all-to-all-start = ((bf16[2,2,256,128]{3,1,0,2:T(2,128)(2,1)}), bf16[2,2,256,128]{3,1,0,2:T(2,128)(2,1)S(1)}, u32[]{:S(2)}, u32[]{:S(2)}) async-start(bf16[2,2,256,128]{3,1,0,2:T(2,128)(2,1)} %copy.16), calls=%async_computation | async-start | bytes 524288 | tf_op jit(solution)/shard_map/all_to_all | solution.py:126
  58.3 24.2 %copy-start.2 = (f32[16,8]{0,1:T(8,128)S(1)}, f32[16,8]{0,1:T(8,128)}, u32[]{:S(2)}) copy-start(f32[16,8]{0,1:T(8,128)} %param.12) | copy-start | bytes 1540
  83.0 1.6 %copy-start = (bf16[4096,256]{1,0:T(8,128)(2,1)S(1)}, bf16[4096,256]{1,0:T(8,128)(2,1)}, u32[]{:S(2)}) copy-start(bf16[4096,256]{1,0:T(8,128)(2,1)} %get-tuple-element.35) | copy-start | bytes 6291460
  85.7 14.6 %copy-start.3 = (s32[2,1,4,128]{3,2,1,0:T(4,128)S(1)}, s32[2,1,4,128]{3,2,1,0:T(4,128)}, u32[]{:S(2)}) copy-start(s32[2,1,4,128]{3,2,1,0:T(4,128)} %param.15) | copy-start | bytes 12292
  85.7 14.8 %copy-start.1 = (s32[2,1,4,128]{3,2,1,0:T(4,128)S(1)}, s32[2,1,4,128]{3,2,1,0:T(4,128)}, u32[]{:S(2)}) copy-start(s32[2,1,4,128]{3,2,1,0:T(4,128)} %param.14) | copy-start | bytes 12292
  87.2 27.2 %all-to-all-start.1 = ((f32[16,1,8,512]{3,2,1,0:T(8,128)}), f32[16,1,8,512]{3,2,1,0:T(8,128)S(1)}, u32[]{:S(2)}, u32[]{:S(2)}) async-start(f32[16,1,8,512]{3,2,1,0:T(8,128)} %maximum_bitcast_fusion.3), calls=%async_computation.1 | async-start | bytes 524288 | tf_op jit(solution)/shard_map/all_to_all | solution.py:20
  115.2 21.1 %all-to-all-start.2 = ((bf16[32,1,8,512]{3,2,1,0:T(8,128)(2,1)}), bf16[32,1,8,512]{3,2,1,0:T(8,128)(2,1)S(1)}, u32[]{:S(2)}, u32[]{:S(2)}) async-start(bf16[32,1,8,512]{3,2,1,0:T(8,128)(2,1)} %broadcast_in_dim.237), calls=%async_computation.2 | async-start | bytes 524288 | tf_op jit(solution)/shard_map/all_to_all | solution.py:32
  136.2 2.3 %copy-start.5 = (s32[1,4]{1,0:T(1,128)S(1)}, s32[1,4]{1,0:T(1,128)}, u32[]{:S(2)}) copy-start(s32[1,4]{1,0:T(1,128)} %param.13) | copy-start | bytes 52
where the time goes:
time: 140 us; the launch traced here: 139 us
  other arithmetic  69.6 us (50%)
  starting transfers between devices  35.6 us (25%)
  waiting for transfers between devices  22.9 us (16%)
  matrix products  5.75 us (4%)
  local copies, waits for them, and re-layouts  4.46 us (3%)
    another operation x4, other arithmetic  64.2 us
    all_to_all x1, waiting for transfers between devices, summed_on_arrival(): lax.all_to_all(pieces, axis, split_axis=0, concat_axis=0, tiled=True)  13.9 us
    all_to_all x1, starting transfers between devices, summed_on_arrival(): lax.all_to_all(pieces, axis, split_axis=0, concat_axis=0, tiled=True)  13.1 us
    all_to_all x1, starting transfers between devices, copy_for_each(): return lax.all_to_all(copies, axis, split_axis=0, concat_axis=0, tiled=True)  12.1 us
    all_to_all x1, starting transfers between devices, local(): lax.all_to_all(pieces, 'col', split_axis=2, concat_axis=3, tiled=True)  10.4 us
    all_to_all x1, waiting for transfers between devices, copy_for_each(): return lax.all_to_all(copies, axis, split_axis=0, concat_axis=0, tiled=True)  8.95 us
  transfers between devices with their start and end apart: 3, of which 2 were waited for; matrix products, arithmetic and copies ran while one was open for 18% of the time, Pallas kernels for 0%

commit v1 on v0

v1 whole, which is shorter than its diff:
```python
import math

import jax
import jax.numpy as jnp
from jax import lax
from jax.experimental import pallas as pl
from jax.experimental.pallas import tpu as pltpu
from jax.sharding import PartitionSpec as P

N_IMG = 65536
S = 256
SCOL = 2
LANES = 128
CHUNK = 512
PARAMS = pltpu.CompilerParams(vmem_limit_bytes=48 * 1024 * 1024)
VMEM = pl.BlockSpec(memory_space=pltpu.VMEM)
SMEM = pl.BlockSpec(memory_space=pltpu.SMEM)
f32 = jnp.float32
bf16 = jnp.bfloat16


def cos_sin(p):
    q = (p + 8192) >> 14
    x = (p - (q << 14)).astype(f32) * (2.0 * math.pi / N_IMG)
    x2 = x * x
    s = x * (1.0 + x2 * (-1.0 / 6 + x2 * (1.0 / 120 + x2 * (-1.0 / 5040 + x2 * (1.0 / 362880)))))
    c = 1.0 + x2 * (-0.5 + x2 * (1.0 / 24 + x2 * (-1.0 / 720 + x2 * (1.0 / 40320))))
    odd = (q & 1) == 1
    a = jnp.where(odd, s, c)
    b = jnp.where(odd, c, s)
    return jnp.where(((q + 1) & 2) == 2, -a, a), jnp.where((q & 2) == 2, -b, b)


def cmul(ac, as_, bc, bs):
    return ac * bc - as_ * bs, as_ * bc + ac * bs


def first_axis_kernel(col_ref, re_ref, im_ref, out_ref, high_ref, table_ref, acc_ref):
    step = pl.program_id(0)
    pixels = lax.broadcasted_iota(jnp.int32, (16, CHUNK), 1) + step * CHUNK
    row = lax.broadcasted_iota(jnp.int32, (16, CHUNK), 0)
    high_c, high_s = cos_sin(row * 16 * pixels)
    high_ref[0] = high_c
    high_ref[1] = high_s
    low_c, low_s = cos_sin(row * pixels)
    for q in range(SCOL):
        off_c, off_s = cos_sin(pixels[:8] * col_ref[q])
        off_c = jnp.concatenate([off_c, off_c], axis=0) * (1.0 / 64)
        off_s = jnp.concatenate([off_s, off_s], axis=0) * (1.0 / 64)
        base_c, base_s = cmul(low_c, low_s, off_c, off_s)
        for h in range(16):
            tc, ts = cmul(base_c, base_s, high_ref[0, h : h + 1, :], high_ref[1, h : h + 1, :])
            table_ref[q * 512 + h * 16 : q * 512 + h * 16 + 16, :] = tc.astype(bf16)
            table_ref[q * 512 + 256 + h * 16 : q * 512 + 256 + h * 16 + 16, :] = ts.astype(bf16)
    image = jnp.concatenate([re_ref[...], im_ref[...]], axis=1)
    product = jnp.dot(table_ref[...], image, preferred_element_type=f32)

    @pl.when(step == 0)
    def _():
        acc_ref[...] = product

    @pl.when(step > 0)
    def _():
        acc_ref[...] += product

    @pl.when(step == pl.num_programs(0) - 1)
    def _():
        for q in range(SCOL):
            cos_part = acc_ref[q * 512 : q * 512 + 256, :]
            sin_part = acc_ref[q * 512 + 256 : q * 512 + 512, :]
            real = (cos_part[:, :LANES] + sin_part[:, LANES:]).reshape(32, 8, LANES)
            imag = (cos_part[:, LANES:] - sin_part[:, :LANES]).reshape(32, 8, LANES)
            out_ref[:, q * 16 : q * 16 + 16, :] = jnp.concatenate([real, imag], axis=1).astype(bf16)


def first_axis(col_offsets, sky_re, sky_im):
    pixels = sky_re.shape[0]
    block = pl.BlockSpec((CHUNK, LANES), lambda i: (i, 0))
    return pl.pallas_call(
        first_axis_kernel,
        grid=(pixels // CHUNK,),
        in_specs=[SMEM, block, block],
        out_specs=pl.BlockSpec((32, 32, LANES), lambda i: (0, 0, 0)),
        out_shape=jax.ShapeDtypeStruct((32, 32, LANES), bf16),
        scratch_shapes=[
            pltpu.VMEM((2, 16, CHUNK), f32),
            pltpu.VMEM((1024, CHUNK), bf16),
            pltpu.VMEM((1024, 256), f32),
        ],
        compiler_params=PARAMS,
        name="first_axis",
    )(col_offsets, sky_re, sky_im)


def second_table_kernel(start_ref, sub_ref, table_ref, shift_ref, high_ref):
    start = start_ref[0]
    cells = lax.broadcasted_iota(jnp.int32, (16, S), 1)
    row = lax.broadcasted_iota(jnp.int32, (16, S), 0)
    low_c, low_s = cos_sin(row * cells)
    low_c = low_c * (1.0 / 256)
    low_s = low_s * (1.0 / 256)
    all_cells = lax.broadcasted_iota(jnp.int32, (256, S), 1)
    all_rows = lax.broadcasted_iota(jnp.int32, (256, S), 0)
    high_c, high_s = cos_sin((start + 16 * all_rows) * all_cells)
    high_ref[0] = high_c
    high_ref[1] = high_s

    def body(i, carry):
        for u in range(8):
            h = i * 8 + u
            tc, ts = cmul(low_c, low_s, high_ref[0, pl.ds(h, 1), :], high_ref[1, pl.ds(h, 1), :])
            table_ref[pl.ds(pl.multiple_of(h * 16, 16), 16), :] = jnp.concatenate([tc, ts], axis=1).astype(bf16)
        return carry

    lax.fori_loop(0, 32, body, 0)
    n_sub = shift_ref.shape[0] // 2
    offs = sub_ref[...]
    for at in range(0, shift_ref.shape[1], 1024):
        y = lax.broadcasted_iota(jnp.int32, (n_sub, 1024), 1) + (start + at)
        c, d = cos_sin(offs * y)
        shift_ref[:n_sub, at : at + 1024] = c
        shift_ref[n_sub:, at : at + 1024] = d


def second_tables(start, sub_offsets, pixels):
    n_sub = sub_offsets.shape[0]
    return pl.pallas_call(
        second_table_kernel,
        in_specs=[SMEM, VMEM],
        out_specs=[VMEM, VMEM],
        out_shape=[
            jax.ShapeDtypeStruct((pixels, 2 * S), bf16),
            jax.ShapeDtypeStruct((2 * n_sub, pixels), f32),
        ],
        scratch_shapes=[pltpu.VMEM((2, 256, S), f32)],
        compiler_params=PARAMS,
        name="second_tables",
    )(start, sub_offsets.reshape(n_sub, 1))


def second_axis_kernel(band_ref, shift_ref, table_ref, out_ref, lhs_ref, acc_ref):
    step = pl.program_id(0)
    n_sub = shift_ref.shape[0] // 2
    for c in range(band_ref.shape[0]):
        lanes = slice(c * LANES, (c + 1) * LANES)
        for q in range(SCOL):
            band = band_ref[c, q * 16 : q * 16 + 16, :].astype(f32)
            re, im = band[:8], band[8:]
            for s in range(q * n_sub // SCOL, (q + 1) * n_sub // SCOL):
                mc = shift_ref[s : s + 1, lanes]
                md = shift_ref[n_sub + s : n_sub + s + 1, lanes]
                both = jnp.concatenate([re * mc + im * md, im * mc - re * md], axis=0)
                lhs_ref[s * 16 : s * 16 + 16, lanes] = both.astype(bf16)
    product = jnp.dot(lhs_ref[...], table_ref[...], preferred_element_type=f32)

    @pl.when(step == 0)
    def _():
        acc_ref[...] = product

    @pl.when(step > 0)
    def _():
        acc_ref[...] += product

    @pl.when(step == pl.num_programs(0) - 1)
    def _():
        total = acc_ref[...].reshape(n_sub, 16, 2 * S)
        re = total[:, :8, :S] + total[:, 8:, S:]
        im = total[:, 8:, :S] - total[:, :8, S:]
        out_ref[:, :S] = re.reshape(n_sub * 8, S).astype(bf16)
        out_ref[:, S:] = im.reshape(n_sub * 8, S).astype(bf16)


def second_axis(band, shift, table):
    pixels = table.shape[0]
    n_sub = shift.shape[0] // 2
    wide = 1024
    return pl.pallas_call(
        second_axis_kernel,
        grid=(pixels // wide,),
        in_specs=[
            pl.BlockSpec((wide // LANES, 32, LANES), lambda i: (i, 0, 0)),
            pl.BlockSpec((2 * n_sub, wide), lambda i: (0, i)),
            pl.BlockSpec((wide, 2 * S), lambda i: (i, 0)),
        ],
        out_specs=pl.BlockSpec((n_sub * 8, 2 * S), lambda i: (0, 0)),
        out_shape=jax.ShapeDtypeStruct((n_sub * 8, 2 * S), bf16),
        scratch_shapes=[
            pltpu.VMEM((n_sub * 16, wide), bf16),
            pltpu.VMEM((n_sub * 16, 2 * S), f32),
        ],
        compiler_params=PARAMS,
        name="second_axis",
    )(band, shift, table)


def own_rows_kernel(terms_ref, out_ref):
    total = terms_ref[0].astype(f32)
    for f in range(1, terms_ref.shape[0]):
        total = total + terms_ref[f].astype(f32)
    rows = total.astype(bf16)
    for c in range(out_ref.shape[0]):
        out_ref[c] = rows


def own_rows(terms, copies):
    return pl.pallas_call(
        own_rows_kernel,
        in_specs=[VMEM],
        out_specs=VMEM,
        out_shape=jax.ShapeDtypeStruct((copies, *terms.shape[1:]), bf16),
        compiler_params=PARAMS,
        name="own_rows",
    )(terms)


def weights_kernel(kernel_ref, cell_ref, frac_ref, row_ref, high_ref, low_ref):
    blocks, slots = cell_ref.shape[1:]
    for b in range(blocks):
        lanes = slice(b * slots, (b + 1) * slots)
        for axis in range(2):
            frac = frac_ref[axis, b : b + 1, :]
            ahead = lax.broadcasted_iota(jnp.int32, (S, slots), 0) - cell_ref[axis, b : b + 1, :]
            spread = jnp.zeros((S, slots), f32)
            for a in range(kernel_ref.shape[1]):
                tap = jnp.zeros((1, slots), f32)
                for o in range(kernel_ref.shape[0]):
                    tap = jnp.where(frac == o, kernel_ref[o, a], tap)
                spread = jnp.where(ahead == a, tap, spread)
            if axis == 0:
                row_ref[:, lanes] = spread.astype(bf16)
            else:
                high = spread.astype(bf16)
                high_ref[:, lanes] = high
                low_ref[:, lanes] = (spread - high.astype(f32)).astype(bf16)


def weights(kernel, cells, fracs):
    total = cells.shape[1] * cells.shape[2]
    shape = jax.ShapeDtypeStruct((S, total), bf16)
    return pl.pallas_call(
        weights_kernel,
        in_specs=[SMEM, VMEM, VMEM],
        out_specs=[VMEM] * 3,
        out_shape=[shape] * 3,
        compiler_params=PARAMS,
        name="weights",
    )(kernel, cells, fracs)


def degrid_kernel(count_ref, grid_ref, row_ref, high_ref, low_ref, re_ref, im_ref):
    blocks, slots = re_ref.shape
    row = row_ref[...].astype(f32)
    for part, out_ref in ((0, re_ref), (1, im_ref)):
        cells = grid_ref[:, part * S : (part + 1) * S]
        sums = jnp.dot(cells, high_ref[...], preferred_element_type=f32)
        sums = sums + jnp.dot(cells, low_ref[...], preferred_element_type=f32)
        values = jnp.sum(sums * row, axis=0, keepdims=True)
        for b in range(blocks):
            live = lax.broadcasted_iota(jnp.int32, (1, slots), 1) < count_ref[b]
            out_ref[b : b + 1, :] = jnp.where(live, values[:, b * slots : (b + 1) * slots], 0.0)


def degrid(counts, grid, row, high, low, blocks, slots):
    shape = jax.ShapeDtypeStruct((blocks, slots), f32)
    return pl.pallas_call(
        degrid_kernel,
        in_specs=[SMEM] + [VMEM] * 4,
        out_specs=[VMEM] * 2,
        out_shape=[shape] * 2,
        compiler_params=PARAMS,
        name="degrid",
    )(counts, grid, row, high, low)


def exchange(x, axis):
    return lax.all_to_all(x, axis, split_axis=0, concat_axis=0, tiled=True)


def local(sky_re, sky_im, col_offsets, sub_offsets, kernel, vis_count, cell_index, frac_index):
    pixels = sky_re.shape[1]
    n_sub = sub_offsets.shape[0]
    col = lax.axis_size("col")
    blocks, slots = cell_index.shape[2:]
    band = exchange(first_axis(col_offsets, sky_re[0], sky_im[0]), "col")
    start = (lax.axis_index("facet") * pixels).astype(jnp.int32).reshape(1)
    table, shift = second_tables(start, sub_offsets, pixels)
    terms = second_axis(band, shift, table)
    arrived = exchange(terms.reshape(n_sub, 8, 2 * S), "facet")
    row, high, low = weights(kernel, cell_index[:, 0], frac_index[:, 0])
    grid = exchange(own_rows(arrived, col), "col").reshape(S, 2 * S)
    vis_re, vis_im = degrid(vis_count[0], grid, row, high, low, blocks, slots)
    return vis_re[None], vis_im[None]


def solution(mesh):
    placed = (
        P("facet", None, "col"),
        P("facet", None, "col"),
        P(),
        P(),
        P(),
        P("facet", "col"),
        P(None, "facet", "col", None),
        P(None, "facet", "col", None),
    )
    return jax.shard_map(
        local,
        mesh=mesh,
        in_specs=placed,
        out_specs=(P("facet", "col", None), P("facet", "col", None)),
        check_vma=False,
    )
```

time: 140 us -> 77.8 us (0.56)
  other arithmetic: 69.6 us -> 0 us
  blocking collectives: 0 us -> 24.9 us
  starting transfers between devices: 35.6 us -> 16.9 us
  Pallas kernels: 0 us -> 15.7 us
  waiting for transfers between devices: 22.9 us -> 11.1 us
  matrix products: 5.75 us -> 0 us
  local copies, waits for them, and re-layouts: 4.46 us -> 8.05 us
    another operation x7 -> x0, other arithmetic: 64.3 us -> none
    all_to_all x0 -> x1, blocking collectives: none -> 24.9 us  [exchange(): return lax.all_to_all(x, axis, split_axis=0, concat_axis=0, tiled=True)]
    all_to_all x3 -> x2, starting transfers between devices: 35.6 us -> 16.9 us  [exchange(): return lax.all_to_all(x, axis, split_axis=0, concat_axis=0, tiled=True)]
    pallas_call x0 -> x6, Pallas kernels: none -> 15.7 us  [the longest x1 7.03 us: first_axis(): pl.pallas_call(first_axis_kernel, grid=(pixels // CHUNK,), in_specs=[SMEM...]
    all_to_all x3 -> x2, waiting for transfers between devices: 22.9 us -> 11.1 us  [exchange(): return lax.all_to_all(x, axis, split_axis=0, concat_axis=0, tiled=True)]
    unnamed x17 -> x19, local copies, waits for them, and re-layouts: 1.34 us -> 7.32 us
    dot_general x5 -> x0, matrix products: 5.75 us -> none  [the longest x2 2.5 us: first_axis(): product = jnp.dot(table, facet_image, preferred_element_type=jnp.float32)]
    slice x4 -> x0, local copies, waits for them, and re-layouts: 1.42 us -> none  [the longest x1 1.31 us: column_table(): col_offsets[column] + spectral]
  transfers between devices with their start and end apart: 3 -> 2, of which waited for: 2 -> 2; matrix products, arithmetic and copies ran while one was open for 18% -> 1% of each run, Pallas kernels for 0% -> 5%
where the time goes in v1:
time: 77.8 us; the launch traced here: 77.4 us
  blocking collectives  24.9 us (32%)
  starting transfers between devices  16.9 us (22%)
  Pallas kernels  15.7 us (20%)
  waiting for transfers between devices  11.1 us (14%)
  local copies, waits for them, and re-layouts  8.05 us (10%)
    all_to_all x1, blocking collectives, exchange(): return lax.all_to_all(x, axis, split_axis=0, concat_axis=0, tiled=True)  24.9 us
    all_to_all x2, starting transfers between devices, exchange(): return lax.all_to_all(x, axis, split_axis=0, concat_axis=0, tiled=True)  16.9 us
    all_to_all x2, waiting for transfers between devices, exchange(): return lax.all_to_all(x, axis, split_axis=0, concat_axis=0, tiled=True)  11.1 us
    unnamed x19, local copies, waits for them, and re-layouts  7.32 us
    pallas_call x1, Pallas kernels, first_axis(): pl.pallas_call(first_axis_kernel, grid=(pixels // CHUNK,), in_specs=[SMEM...  7.03 us
    pallas_call x1, Pallas kernels, second_tables(): pl.pallas_call(second_table_kernel, in_specs=[SMEM, VMEM], out_specs=[VME...  2.52 us
    pallas_call x1, Pallas kernels, second_axis(): pl.pallas_call(second_axis_kernel, grid=(pixels // wide,), in_specs=[pl.B...  2.15 us
    pallas_call x1, Pallas kernels, weights(): pl.pallas_call(weights_kernel, in_specs=[SMEM, VMEM, VMEM], out_specs=[VM...  1.68 us
  transfers between devices with their start and end apart: 2, of which 2 were waited for; matrix products, arithmetic and copies ran while one was open for 1% of the time, Pallas kernels for 5%

profile of v1, /device:TPU:1, one launch (start us, length us, event | category | flops | bytes accessed | tf_op | source)
XLA Modules:
  0.0 77.4 jit_solution(11254088668972584642)
XLA Ops:
  0.6 0.0 copy-start.2
  0.6 1.2 %copy-done.2 = bf16[1,4096,128]{2,1,0:T(8,128)(2,1)S(1)} copy-done((bf16[1,4096,128]{2,1,0:T(8,128)(2,1)S(1)}, bf16[1,4096,128]{2,1,0:T(8,128)(2,1)}, u32[]{:S(2)}) %copy-start.2) | copy-done | bytes 1048600
  1.9 1.2 %copy-done.3 = bf16[1,4096,128]{2,1,0:T(8,128)(2,1)S(1)} copy-done((bf16[1,4096,128]{2,1,0:T(8,128)(2,1)S(1)}, bf16[1,4096,128]{2,1,0:T(8,128)(2,1)}, u32[]{:S(2)}) %copy-start.3) | copy-done | bytes 1048600
  3.1 0.7 copy-done.6
  3.8 7.0 %first_axis.1 = bf16[32,32,128]{2,1,0:T(8,128)(2,1)} custom-call(s32[2]{0:T(128)S(1)} %copy-done.6, bf16[4096,128]{1,0:T(8,128)(2,1)S(1)} %bitcast.11, bf16[4096,128]{1,0:T(8,128)(2,1)S(1)} %bitcast.12), custom_call_target="tpu_custom_call" | custom-call | tf_op jit(solution)/shard_map/first_axis/pallas_call | solution.py:79
  10.8 10.4 %all-to-all-start = ((bf16[32,32,128]{2,1,0:T(8,128)(2,1)}), bf16[32,32,128]{2,1,0:T(8,128)(2,1)S(1)}, u32[]{:S(2)}, u32[]{:S(2)}) async-start(bf16[32,32,128]{2,1,0:T(8,128)(2,1)} %first_axis.1), calls=%async_computation | async-start | bytes 524288 | tf_op jit(solution)/shard_map/all_to_all | solution.py:276
  21.2 0.7 copy.10.sub_ref
  21.9 2.5 %second_tables.1 = (bf16[4096,512]{1,0:T(8,128)(2,1)S(1)}, f32[32,4096]{1,0:T(8,128)S(1)}) custom-call(s32[1]{0:T(128)} %bitcast.3.start_ref, s32[16,1]{1,0:T(8,128)S(1)} %copy.10.sub_ref), custom_call_target="tpu_custom_call" | custom-call | tf_op jit(solution)/shard_map/second_tables/pallas_call | solution.py:127
  24.5 0.0 copy-start
  24.5 1.9 %copy-done = bf16[4096,512]{1,0:T(8,128)(2,1)} copy-done((bf16[4096,512]{1,0:T(8,128)(2,1)}, bf16[4096,512]{1,0:T(8,128)(2,1)S(1)}, u32[]{:S(2)}) %copy-start) | copy-done | bytes 4194328
  26.4 3.9 %all-to-all-done.band_ref = bf16[32,32,128]{2,1,0:T(8,128)(2,1)S(1)} async-done(((bf16[32,32,128]{2,1,0:T(8,128)(2,1)}), bf16[32,32,128]{2,1,0:T(8,128)(2,1)S(1)}, u32[]{:S(2)}, u32[]{:S(2)}) %all-to-all-start) | async-done | bytes 262176 | tf_op jit(solution)/shard_map/all_to_all | solution.py:276
  30.3 2.2 %copy-done.1 = bf16[4096,512]{1,0:T(8,128)(2,1)S(1)} copy-done((bf16[4096,512]{1,0:T(8,128)(2,1)S(1)}, bf16[4096,512]{1,0:T(8,128)(2,1)}, u32[]{:S(2)}) %copy-start.1) | copy-done | bytes 4194328
  32.5 2.2 %second_axis.1 = bf16[128,512]{1,0:T(8,128)(2,1)S(1)} custom-call(bf16[32,32,128]{2,1,0:T(8,128)(2,1)S(1)} %all-to-all-done.band_ref, f32[32,4096]{1,0:T(8,128)S(1)} %get-tuple-element.9.shift_ref, bf16[4096,512]{1,0:T(8,128)(2,1)S(1)} %copy-done.1), custom_call_target="tpu_custom_call" | custom-call | tf_op jit(solution)/shard_map/second_axis/pallas_call | solution.py:177
  34.6 24.9 %all_to_all.15.terms_ref = bf16[16,8,512]{2,1,0:T(8,128)(2,1)S(1)} all-to-all(bf16[16,8,512]{2,1,0:T(8,128)(2,1)S(1)} %bitcast.14), channel_id=1, replica_groups=mesh['facet'=16,'col'=32] {'facet'}, dimensions={0} | all-to-all | bytes 262144 | tf_op jit(solution)/shard_map/all_to_all | solution.py:276
  59.6 0.7 own_rows.1
  60.3 6.5 %all-to-all-start.2 = ((bf16[32,8,512]{2,1,0:T(8,128)(2,1)}), bf16[32,8,512]{2,1,0:T(8,128)(2,1)S(1)}, u32[]{:S(2)}, u32[]{:S(2)}) async-start(bf16[32,8,512]{2,1,0:T(8,128)(2,1)} %own_rows.1), calls=%async_computation.2 | async-start | bytes 524288 | tf_op jit(solution)/shard_map/all_to_all | solution.py:276
  66.8 0.0 copy-done.8
  66.8 0.1 copy.11.kernel_ref
  66.9 0.0 copy-done.4
  66.9 0.0 copy-done.5
  66.9 1.7 %weights.1 = (bf16[256,512]{1,0:T(8,128)(2,1)S(1)}, bf16[256,512]{1,0:T(8,128)(2,1)S(1)}, bf16[256,512]{1,0:T(8,128)(2,1)S(1)}) custom-call(f32[16,8]{1,0:T(8,128)S(1)} %copy.11.kernel_ref, s32[2,4,128]{2,1,0:T(4,128)S(1)} %bitcast.15, s32[2,4,128]{2,1,0:T(4,128)S(1)} %bitcast.16), custom_call_target="tpu_custom_call" | custom-call | tf_op jit(solution)/shard_map/weights/pallas_call | solution.py:240
  68.6 7.2 %all-to-all-done.2 = bf16[32,8,512]{2,1,0:T(8,128)(2,1)S(1)} async-done(((bf16[32,8,512]{2,1,0:T(8,128)(2,1)}), bf16[32,8,512]{2,1,0:T(8,128)(2,1)S(1)}, u32[]{:S(2)}, u32[]{:S(2)}) %all-to-all-start.2) | async-done | bytes 262176 | tf_op jit(solution)/shard_map/all_to_all | solution.py:276
  75.8 0.0 copy-done.7
  75.8 1.6 %degrid.1 = (f32[4,128]{1,0:T(4,128)}, f32[4,128]{1,0:T(4,128)}) custom-call(s32[4]{0:T(128)S(1)} %bitcast.17, bf16[256,512]{1,0:T(8,128)(2,1)S(1)} %bitcast.13, bf16[256,512]{1,0:T(8,128)(2,1)S(1)} %get-tuple-element.11.row_ref, bf16[256,512]{1,0:T(8,128)(2,1)S(1)} %get-tuple-element.12.high_ref, bf16[256,512]{1,0:T(8,128)(2,1)S(1)} %get-tuple-element.13.low_ref), custom_call_target="tpu_custom_call" | custom-call | tf_op jit(solution)/shard_map/degrid/pallas_call | solution.py:265
  (7 shorter events, 0.0 us)
Async XLA Ops:
  0.6 1.2 %copy-start.2 = (bf16[1,4096,128]{2,1,0:T(8,128)(2,1)S(1)}, bf16[1,4096,128]{2,1,0:T(8,128)(2,1)}, u32[]{:S(2)}) copy-start(bf16[1,4096,128]{2,1,0:T(8,128)(2,1)} %param.8) | copy-start | bytes 3145732
  1.9 1.2 %copy-start.3 = (bf16[1,4096,128]{2,1,0:T(8,128)(2,1)S(1)}, bf16[1,4096,128]{2,1,0:T(8,128)(2,1)}, u32[]{:S(2)}) copy-start(bf16[1,4096,128]{2,1,0:T(8,128)(2,1)} %param.9) | copy-start | bytes 3145732
  3.1 0.7 copy-start.6
  3.7 63.1 %copy-start.8 = (f32[16,8]{0,1:T(8,128)S(1)}, f32[16,8]{0,1:T(8,128)}, u32[]{:S(2)}) copy-start(f32[16,8]{0,1:T(8,128)} %param.12) | copy-start | bytes 1540
  3.7 63.2 %copy-start.4 = (s32[2,1,4,128]{3,2,1,0:T(4,128)S(1)}, s32[2,1,4,128]{3,2,1,0:T(4,128)}, u32[]{:S(2)}) copy-start(s32[2,1,4,128]{3,2,1,0:T(4,128)} %param.14) | copy-start | bytes 12292
  3.7 63.2 %copy-start.5 = (s32[2,1,4,128]{3,2,1,0:T(4,128)S(1)}, s32[2,1,4,128]{3,2,1,0:T(4,128)}, u32[]{:S(2)}) copy-start(s32[2,1,4,128]{3,2,1,0:T(4,128)} %param.15) | copy-start | bytes 12292
  3.7 72.1 %copy-start.7 = (s32[1,4]{1,0:T(1,128)S(1)}, s32[1,4]{1,0:T(1,128)}, u32[]{:S(2)}) copy-start(s32[1,4]{1,0:T(1,128)} %param.13) | copy-start | bytes 52
  10.8 19.5 %all-to-all-start = ((bf16[32,32,128]{2,1,0:T(8,128)(2,1)}), bf16[32,32,128]{2,1,0:T(8,128)(2,1)S(1)}, u32[]{:S(2)}, u32[]{:S(2)}) async-start(bf16[32,32,128]{2,1,0:T(8,128)(2,1)} %first_axis.1), calls=%async_computation | async-start | bytes 524288 | tf_op jit(solution)/shard_map/all_to_all | solution.py:276
  24.5 2.0 %copy-start = (bf16[4096,512]{1,0:T(8,128)(2,1)}, bf16[4096,512]{1,0:T(8,128)(2,1)S(1)}, u32[]{:S(2)}) copy-start(bf16[4096,512]{1,0:T(8,128)(2,1)S(1)} %get-tuple-element.10.table_ref) | copy-start | bytes 12582916
  30.3 2.2 %copy-start.1 = (bf16[4096,512]{1,0:T(8,128)(2,1)S(1)}, bf16[4096,512]{1,0:T(8,128)(2,1)}, u32[]{:S(2)}) copy-start(bf16[4096,512]{1,0:T(8,128)(2,1)} %copy-done) | copy-start | bytes 12582916
  60.3 15.5 %all-to-all-start.2 = ((bf16[32,8,512]{2,1,0:T(8,128)(2,1)}), bf16[32,8,512]{2,1,0:T(8,128)(2,1)S(1)}, u32[]{:S(2)}, u32[]{:S(2)}) async-start(bf16[32,8,512]{2,1,0:T(8,128)(2,1)} %own_rows.1), calls=%async_computation.2 | async-start | bytes 524288 | tf_op jit(solution)/shard_map/all_to_all | solution.py:276

commit v2 on v1

v2 whole, which is shorter than its diff:
```python
import math

import jax
import jax.numpy as jnp
from jax import lax
from jax.experimental import pallas as pl
from jax.experimental.pallas import tpu as pltpu
from jax.sharding import PartitionSpec as P

N_IMG = 65536
S = 256
SCOL = 2
LANES = 128
PAIRS = 4
LOADS = 4
READY = 3072
PARAMS = pltpu.CompilerParams(vmem_limit_bytes=16 * 1024 * 1024)
MIDDLE = pltpu.CompilerParams(vmem_limit_bytes=24 * 1024 * 1024)
WIDE = pltpu.CompilerParams(vmem_limit_bytes=60 * 1024 * 1024)
VMEM = pl.BlockSpec(memory_space=pltpu.VMEM)
SMEM = pl.BlockSpec(memory_space=pltpu.SMEM)
HBM = pl.BlockSpec(memory_space=pltpu.HBM)
f32 = jnp.float32
bf16 = jnp.bfloat16


def cos_sin(p):
    q = (p + 8192) >> 14
    x = (p - (q << 14)).astype(f32) * (2.0 * math.pi / N_IMG)
    x2 = x * x
    s = x * (1.0 + x2 * (-1.0 / 6 + x2 * (1.0 / 120 + x2 * (-1.0 / 5040 + x2 * (1.0 / 362880)))))
    c = 1.0 + x2 * (-0.5 + x2 * (1.0 / 24 + x2 * (-1.0 / 720 + x2 * (1.0 / 40320))))
    odd = (q & 1) == 1
    a = jnp.where(odd, s, c)
    b = jnp.where(odd, c, s)
    return jnp.where(((q + 1) & 2) == 2, -a, a), jnp.where((q & 2) == 2, -b, b)


def cmul(ac, as_, bc, bs):
    return ac * bc - as_ * bs, as_ * bc + ac * bs


def row_phases(mult, scale, blocks):
    lane = lax.broadcasted_iota(jnp.int32, (8, LANES), 1)
    low_c, low_s = cos_sin(mult * lane)
    high_c, high_s = cos_sin(mult * (lane * LANES))
    low_c, low_s = low_c * scale, low_s * scale
    return [cmul(low_c, low_s, high_c[:, b : b + 1], high_s[:, b : b + 1]) for b in range(blocks)]


def first_axis_kernel(col_hbm, re_hbm, im_hbm, out_ref, col_ref, sky_ref, base_ref, step_ref, sem):
    pixels = re_hbm.shape[0]
    blocks = pixels // LANES
    part = pixels // LOADS
    col_copy = pltpu.make_async_copy(col_hbm, col_ref, sem.at[0])
    col_copy.start()
    copies = []
    for i in range(LOADS):
        for k, src in enumerate((re_hbm, im_hbm)):
            rows = pl.ds(i * part, part)
            dst = sky_ref.at[rows, pl.ds(k * LANES, LANES)]
            copies.append(pltpu.make_async_copy(src.at[rows], dst, sem.at[1 + 2 * i + k]))
            copies[-1].start()
    row = lax.broadcasted_iota(jnp.int32, (8, LANES), 0)
    near = row_phases(row * 8, 1.0, blocks)
    far = row_phases(row * 64, 1.0, blocks)
    for b in range(blocks):
        lanes = slice(b * LANES, (b + 1) * LANES)
        (near_c, near_s), (far_c, far_s) = near[b], far[b]
        next_c, next_s = cmul(near_c, near_s, far_c[1:2], far_s[1:2])
        for k, rows in enumerate(((near_c, next_c, far_c), (near_s, next_s, far_s))):
            for i in range(3):
                step_ref[k, 8 * i : 8 * i + 8, lanes] = rows[i]
    col_copy.wait()
    for q in range(SCOL):
        middle = row_phases(row + (col_ref[q] + 128), 1.0 / 64, blocks)
        for b in range(blocks):
            lanes = slice(b * LANES, (b + 1) * LANES)
            base_ref[q, 0, :, lanes] = middle[b][0]
            base_ref[q, 1, :, lanes] = middle[b][1]

    def table_rows(q, first):
        cols = []
        for b in range(blocks):
            lanes = slice(b * LANES, (b + 1) * LANES)
            bc, bs = base_ref[q, 0, :, lanes], base_ref[q, 1, :, lanes]
            up_c, up_s, down_c, down_s = [], [], [], []
            for d in range(first, first + PAIRS):
                at = 18 if d == 16 else d
                hc, hs = step_ref[0, at : at + 1, lanes], step_ref[1, at : at + 1, lanes]
                cc, ss, sc, cs = bc * hc, bs * hs, bs * hc, bc * hs
                up_c.append(bc if d == 16 else cc - ss)
                up_s.append(bs if d == 16 else sc + cs)
                down_c.append(cc + ss)
                down_s.append(sc - cs)
            cols.append(jnp.concatenate(up_c + up_s + down_c + down_s, axis=0).astype(bf16))
        return jnp.concatenate(cols, axis=1)

    for copy in copies:
        copy.wait()
    for q in range(SCOL):
        for first in range(1, 17, PAIRS):
            product = jnp.dot(table_rows(q, first), sky_ref[...], preferred_element_type=f32)
            side = 8 * PAIRS
            for k in range(2):
                c = product[2 * k * side : (2 * k + 1) * side]
                s = product[(2 * k + 1) * side : (2 * k + 2) * side]
                real = c[:, :LANES] + s[:, LANES:]
                imag = c[:, LANES:] - s[:, :LANES]
                for t in range(PAIRS):
                    d = first + t
                    group = 16 - d if k == 1 else 16 if d == 16 else 16 + d
                    rows = slice(8 * t, 8 * t + 8)
                    both = jnp.concatenate([real[rows], imag[rows]], axis=0)
                    out_ref[group, q * 16 : q * 16 + 16, :] = both.astype(bf16)


def first_axis(col_offsets, sky_re, sky_im):
    pixels = sky_re.shape[0]
    return pl.pallas_call(
        first_axis_kernel,
        in_specs=[HBM] * 3,
        out_specs=VMEM,
        out_shape=jax.ShapeDtypeStruct((32, 32, LANES), bf16),
        scratch_shapes=[
            pltpu.SMEM((SCOL,), jnp.int32),
            pltpu.VMEM((pixels, 2 * LANES), bf16),
            pltpu.VMEM((SCOL, 2, 8, pixels), f32),
            pltpu.VMEM((2, 24, pixels), f32),
            pltpu.SemaphoreType.DMA((1 + 2 * LOADS,)),
        ],
        compiler_params=WIDE,
        name="first_axis",
    )(col_offsets, sky_re, sky_im)


def table_blocks(start, step_ref, blocks):
    cells = lax.broadcasted_iota(jnp.int32, (8, S), 1)
    row = lax.broadcasted_iota(jnp.int32, (8, S), 0)
    for i in range(2):
        c, s = cos_sin((row + 8 * i) * 8 * cells)
        step_ref[0, 8 * i : 8 * i + 8, :] = c
        step_ref[1, 8 * i : 8 * i + 8, :] = s
    last = cos_sin(cells[:1] * 128)
    base_c, base_s = cos_sin((row + 128) * cells)
    base_c, base_s = base_c * (1.0 / 256), base_s * (1.0 / 256)
    block = lax.broadcasted_iota(jnp.int32, (16, S), 0)
    block_c, block_s = cos_sin((start + 256 * block) * lax.broadcasted_iota(jnp.int32, (16, S), 1))
    made = []
    for g in blocks:
        bc, bs = cmul(base_c, base_s, block_c[g : g + 1], block_s[g : g + 1])
        up, down = [], []
        for d in range(1, 17):
            hc, hs = last if d == 16 else (step_ref[0, d : d + 1, :], step_ref[1, d : d + 1, :])
            cc, ss, sc, cs = bc * hc, bs * hs, bs * hc, bc * hs
            if d < 16:
                up.append(jnp.concatenate([cc - ss, sc + cs], axis=1))
            down.append(jnp.concatenate([cc + ss, sc - cs], axis=1))
        rows = down[::-1] + [jnp.concatenate([bc, bs], axis=1)] + up
        made.append(jnp.concatenate(rows, axis=0).astype(bf16))
    return made


def second_table_kernel(start_ref, table_ref, step_ref):
    blocks = range(table_ref.shape[0] // 256)
    for g, made in zip(blocks, table_blocks(start_ref[0], step_ref, blocks)):
        table_ref[g * 256 : (g + 1) * 256, :] = made


def second_table(start, rows):
    return pl.pallas_call(
        second_table_kernel,
        in_specs=[SMEM],
        out_specs=VMEM,
        out_shape=jax.ShapeDtypeStruct((rows, 2 * S), bf16),
        scratch_shapes=[pltpu.VMEM((2, 16, S), f32)],
        compiler_params=PARAMS,
        name="second_table",
    )(start)


def second_axis_kernel(start_ref, sub_ref, band_ref, ready_ref, out_ref, shift_ref, table_ref, step_ref):
    n_sub = sub_ref.shape[0]
    chunks = band_ref.shape[0]
    per = n_sub // SCOL
    start = start_ref[0]
    ready = ready_ref.shape[0]
    row = lax.broadcasted_iota(jnp.int32, (n_sub, LANES), 0)
    lane = lax.broadcasted_iota(jnp.int32, (n_sub, LANES), 1)
    offs = jnp.zeros((n_sub, LANES), jnp.int32)
    for s in range(n_sub):
        offs = jnp.where(row == s, sub_ref[s], offs)
    low_c, low_s = cos_sin(offs * lane)
    high_c, high_s = cos_sin(offs * (lane * LANES + start))
    for b in range(chunks):
        lanes = slice(b * LANES, (b + 1) * LANES)
        c, d = cmul(low_c, low_s, high_c[:, b : b + 1], high_s[:, b : b + 1])
        shift_ref[0, :, lanes] = c
        shift_ref[1, :, lanes] = d
    for g, made in enumerate(table_blocks(start, step_ref, range(ready // 256, chunks // 2))):
        table_ref[g * 256 : (g + 1) * 256, :] = made

    def shifted(q):
        cols = []
        for c in range(chunks):
            lanes = slice(c * LANES, (c + 1) * LANES)
            band = band_ref[c, q * 16 : q * 16 + 16, :].astype(f32)
            re, im = band[:8], band[8:]
            rows = []
            for s in range(q * per, (q + 1) * per):
                mc = shift_ref[0, s : s + 1, lanes]
                md = shift_ref[1, s : s + 1, lanes]
                rows += [re * mc + im * md, im * mc - re * md]
            cols.append(jnp.concatenate(rows, axis=0).astype(bf16))
        return jnp.concatenate(cols, axis=1)

    left = jnp.concatenate([shifted(q) for q in range(SCOL)], axis=0)
    product = jnp.dot(left[:, :ready], ready_ref[...], preferred_element_type=f32)
    product = product + jnp.dot(left[:, ready:], table_ref[...], preferred_element_type=f32)
    product = product.reshape(n_sub, 16, 2 * S)
    re = product[:, :8, :S] + product[:, 8:, S:]
    im = product[:, 8:, :S] - product[:, :8, S:]
    out_ref[:, :S] = re.reshape(n_sub * 8, S).astype(bf16)
    out_ref[:, S:] = im.reshape(n_sub * 8, S).astype(bf16)


def second_axis(start, sub_offsets, band, ready):
    n_sub = sub_offsets.shape[0]
    pixels = band.shape[0] * LANES
    return pl.pallas_call(
        second_axis_kernel,
        in_specs=[SMEM, SMEM, VMEM, VMEM],
        out_specs=VMEM,
        out_shape=jax.ShapeDtypeStruct((n_sub * 8, 2 * S), bf16),
        scratch_shapes=[
            pltpu.VMEM((2, n_sub, pixels), f32),
            pltpu.VMEM((pixels - ready.shape[0], 2 * S), bf16),
            pltpu.VMEM((2, 16, S), f32),
        ],
        compiler_params=MIDDLE,
        name="second_axis",
    )(start, sub_offsets, band, ready)


def own_rows_kernel(terms_ref, out_ref):
    total = terms_ref[0].astype(f32)
    for f in range(1, terms_ref.shape[0]):
        total = total + terms_ref[f].astype(f32)
    rows = total.astype(bf16)
    for c in range(out_ref.shape[0]):
        out_ref[c] = rows


def own_rows(terms, copies):
    return pl.pallas_call(
        own_rows_kernel,
        in_specs=[VMEM],
        out_specs=VMEM,
        out_shape=jax.ShapeDtypeStruct((copies, *terms.shape[1:]), bf16),
        compiler_params=PARAMS,
        name="own_rows",
    )(terms)


def weights_kernel(kernel_ref, cell_ref, frac_ref, row_ref, high_ref, low_ref):
    blocks, slots = cell_ref.shape[1:]
    for b in range(blocks):
        lanes = slice(b * slots, (b + 1) * slots)
        for axis in range(2):
            frac = frac_ref[axis, b : b + 1, :]
            ahead = lax.broadcasted_iota(jnp.int32, (S, slots), 0) - cell_ref[axis, b : b + 1, :]
            spread = jnp.zeros((S, slots), f32)
            for a in range(kernel_ref.shape[1]):
                tap = jnp.zeros((1, slots), f32)
                for o in range(kernel_ref.shape[0]):
                    tap = jnp.where(frac == o, kernel_ref[o, a], tap)
                spread = jnp.where(ahead == a, tap, spread)
            if axis == 0:
                row_ref[:, lanes] = spread.astype(bf16)
            else:
                high = spread.astype(bf16)
                high_ref[:, lanes] = high
                low_ref[:, lanes] = (spread - high.astype(f32)).astype(bf16)


def weights(kernel, cells, fracs):
    total = cells.shape[1] * cells.shape[2]
    shape = jax.ShapeDtypeStruct((S, total), bf16)
    return pl.pallas_call(
        weights_kernel,
        in_specs=[SMEM, VMEM, VMEM],
        out_specs=[VMEM] * 3,
        out_shape=[shape] * 3,
        compiler_params=PARAMS,
        name="weights",
    )(kernel, cells, fracs)


def degrid_kernel(count_ref, grid_ref, row_ref, high_ref, low_ref, re_ref, im_ref):
    blocks, slots = re_ref.shape
    row = row_ref[...].astype(f32)
    for part, out_ref in ((0, re_ref), (1, im_ref)):
        cells = grid_ref[:, part * S : (part + 1) * S]
        sums = jnp.dot(cells, high_ref[...], preferred_element_type=f32)
        sums = sums + jnp.dot(cells, low_ref[...], preferred_element_type=f32)
        values = jnp.sum(sums * row, axis=0, keepdims=True)
        for b in range(blocks):
            live = lax.broadcasted_iota(jnp.int32, (1, slots), 1) < count_ref[b]
            out_ref[b : b + 1, :] = jnp.where(live, values[:, b * slots : (b + 1) * slots], 0.0)


def degrid(counts, grid, row, high, low, blocks, slots):
    shape = jax.ShapeDtypeStruct((blocks, slots), f32)
    return pl.pallas_call(
        degrid_kernel,
        in_specs=[SMEM] + [VMEM] * 4,
        out_specs=[VMEM] * 2,
        out_shape=[shape] * 2,
        compiler_params=PARAMS,
        name="degrid",
    )(counts, grid, row, high, low)


def exchange(x, axis):
    return lax.all_to_all(x, axis, split_axis=0, concat_axis=0, tiled=True)


def local(sky_re, sky_im, col_offsets, sub_offsets, kernel, vis_count, cell_index, frac_index):
    pixels = sky_re.shape[1]
    n_sub = sub_offsets.shape[0]
    col = lax.axis_size("col")
    blocks, slots = cell_index.shape[2:]
    band = exchange(first_axis(col_offsets, sky_re[0], sky_im[0]), "col")
    start = (lax.axis_index("facet") * pixels).astype(jnp.int32).reshape(1)
    terms = second_axis(start, sub_offsets, band, second_table(start, READY))
    arrived = exchange(terms.reshape(n_sub, 8, 2 * S), "facet")
    row, high, low = weights(kernel, cell_index[:, 0], frac_index[:, 0])
    grid = exchange(own_rows(arrived, col), "col").reshape(S, 2 * S)
    vis_re, vis_im = degrid(vis_count[0], grid, row, high, low, blocks, slots)
    return vis_re[None], vis_im[None]


def solution(mesh):
    placed = (
        P("facet", None, "col"),
        P("facet", None, "col"),
        P(),
        P(),
        P(),
        P("facet", "col"),
        P(None, "facet", "col", None),
        P(None, "facet", "col", None),
    )
    return jax.shard_map(
        local,
        mesh=mesh,
        in_specs=placed,
        out_specs=(P("facet", "col", None), P("facet", "col", None)),
        check_vma=False,
    )
```

time: 77.8 us -> 69.8 us (0.90)
  local copies, waits for them, and re-layouts: 8.05 us -> 0.1 us
  waiting for transfers between devices: 11.1 us -> 15.2 us
  Pallas kernels: 15.7 us -> 11.7 us
    unnamed x19 -> x11, local copies, waits for them, and re-layouts: 7.32 us -> 0.1 us
    all_to_all x2, waiting for transfers between devices: 11.1 us -> 15.2 us  [exchange(): return lax.all_to_all(x, axis, split_axis=0, concat_axis=0, tiled=True)]
    pallas_call x3, Pallas kernels: 11.7 us -> 7.73 us  [the longest x1 4.67 us: first_axis(): pl.pallas_call(first_axis_kernel, in_specs=[HBM] * 3, out_specs=VMEM, out...]
  transfers between devices with their start and end apart: 2 -> 2, of which waited for: 2 -> 2; matrix products, arithmetic and copies ran while one was open for 1% -> 0% of each run, Pallas kernels for 5% -> 4%
where the time goes in v2:
time: 69.8 us; the launch traced here: 69.5 us
  blocking collectives  24.9 us (36%)
  starting transfers between devices  16.8 us (24%)
  waiting for transfers between devices  15.2 us (22%)
  Pallas kernels  11.7 us (17%)
  between operations  0.73 us (1%)
    all_to_all x1, blocking collectives, exchange(): return lax.all_to_all(x, axis, split_axis=0, concat_axis=0, tiled=True)  24.9 us
    all_to_all x2, starting transfers between devices, exchange(): return lax.all_to_all(x, axis, split_axis=0, concat_axis=0, tiled=True)  16.8 us
    all_to_all x2, waiting for transfers between devices, exchange(): return lax.all_to_all(x, axis, split_axis=0, concat_axis=0, tiled=True)  15.2 us
    pallas_call x1, Pallas kernels, first_axis(): pl.pallas_call(first_axis_kernel, in_specs=[HBM] * 3, out_specs=VMEM, out...  4.67 us
    pallas_call x1, Pallas kernels, second_axis(): pl.pallas_call(second_axis_kernel, in_specs=[SMEM, SMEM, VMEM, VMEM], out...  1.97 us
    pallas_call x1, Pallas kernels, weights(): pl.pallas_call(weights_kernel, in_specs=[SMEM, VMEM, VMEM], out_specs=[VM...  1.68 us
    pallas_call x1, Pallas kernels, degrid(): pl.pallas_call(degrid_kernel, in_specs=[SMEM] + [VMEM] * 4, out_specs=[VM...  1.57 us
  transfers between devices with their start and end apart: 2, of which 2 were waited for; matrix products, arithmetic and copies ran while one was open for 0% of the time, Pallas kernels for 4%

profile of v2, /device:TPU:1, one launch (start us, length us, event | category | flops | bytes accessed | tf_op | source)
XLA Modules:
  0.0 69.5 jit_solution(15861662745769128468)
XLA Ops:
  0.6 0.0 copy-start.2
  0.6 4.7 %first_axis.1 = bf16[32,32,128]{2,1,0:T(8,128)(2,1)} custom-call(s32[2]{0:T(128)} %col_hbm.1, bf16[4096,128]{1,0:T(8,128)(2,1)} %bitcast.15, bf16[4096,128]{1,0:T(8,128)(2,1)} %bitcast.16), custom_call_target="tpu_custom_call" | custom-call | tf_op jit(solution)/shard_map/first_axis/pallas_call | solution.py:120
  5.3 10.4 %all-to-all-start = ((bf16[32,32,128]{2,1,0:T(8,128)(2,1)}), bf16[32,32,128]{2,1,0:T(8,128)(2,1)S(1)}, u32[]{:S(2)}, u32[]{:S(2)}) async-start(bf16[32,32,128]{2,1,0:T(8,128)(2,1)} %first_axis.1), calls=%async_computation | async-start | bytes 524288 | tf_op jit(solution)/shard_map/all_to_all | solution.py:325
  15.7 1.1 %second_table.1.ready_ref = bf16[3072,512]{1,0:T(8,128)(2,1)S(1)} custom-call(s32[1]{0:T(128)} %bitcast.1.start_ref), custom_call_target="tpu_custom_call" | custom-call | tf_op jit(solution)/shard_map/second_table/pallas_call | solution.py:171
  16.8 0.0 copy-start.4
  16.8 0.0 copy-start
  16.9 0.0 copy-start.1
  16.9 0.0 copy-start.3
  16.9 7.9 %all-to-all-done.band_ref = bf16[32,32,128]{2,1,0:T(8,128)(2,1)S(1)} async-done(((bf16[32,32,128]{2,1,0:T(8,128)(2,1)}), bf16[32,32,128]{2,1,0:T(8,128)(2,1)S(1)}, u32[]{:S(2)}, u32[]{:S(2)}) %all-to-all-start) | async-done | bytes 262176 | tf_op jit(solution)/shard_map/all_to_all | solution.py:325
  24.8 0.0 copy-done.2
  24.8 2.0 %second_axis.1 = bf16[128,512]{1,0:T(8,128)(2,1)S(1)} custom-call(s32[1]{0:T(128)} %bitcast.1.start_ref, s32[16]{0:T(128)S(1)} %copy-done.2, bf16[32,32,128]{2,1,0:T(8,128)(2,1)S(1)} %all-to-all-done.band_ref, bf16[3072,512]{1,0:T(8,128)(2,1)S(1)} %second_table.1.ready_ref), custom_call_target="tpu_custom_call" | custom-call | tf_op jit(solution)/shard_map/second_axis/pallas_call | solution.py:230
  26.8 24.9 %all_to_all.15.terms_ref = bf16[16,8,512]{2,1,0:T(8,128)(2,1)S(1)} all-to-all(bf16[16,8,512]{2,1,0:T(8,128)(2,1)S(1)} %bitcast.11), channel_id=1, replica_groups=mesh['facet'=16,'col'=32] {'facet'}, dimensions={0} | all-to-all | bytes 262144 | tf_op jit(solution)/shard_map/all_to_all | solution.py:325
  51.8 0.7 %own_rows.1 = bf16[32,8,512]{2,1,0:T(8,128)(2,1)} custom-call(bf16[16,8,512]{2,1,0:T(8,128)(2,1)S(1)} %all_to_all.15.terms_ref), custom_call_target="tpu_custom_call" | custom-call | tf_op jit(solution)/shard_map/own_rows/pallas_call | solution.py:255
  52.5 6.4 %all-to-all-start.2 = ((bf16[32,8,512]{2,1,0:T(8,128)(2,1)}), bf16[32,8,512]{2,1,0:T(8,128)(2,1)S(1)}, u32[]{:S(2)}, u32[]{:S(2)}) async-start(bf16[32,8,512]{2,1,0:T(8,128)(2,1)} %own_rows.1), calls=%async_computation.2 | async-start | bytes 524288 | tf_op jit(solution)/shard_map/all_to_all | solution.py:325
  58.9 0.0 copy-done.4
  58.9 0.1 copy.10.kernel_ref
  59.0 0.0 copy-done
  59.0 0.0 copy-done.1
  59.0 1.7 %weights.1 = (bf16[256,512]{1,0:T(8,128)(2,1)S(1)}, bf16[256,512]{1,0:T(8,128)(2,1)S(1)}, bf16[256,512]{1,0:T(8,128)(2,1)S(1)}) custom-call(f32[16,8]{1,0:T(8,128)S(1)} %copy.10.kernel_ref, s32[2,4,128]{2,1,0:T(4,128)S(1)} %bitcast.12, s32[2,4,128]{2,1,0:T(4,128)S(1)} %bitcast.13), custom_call_target="tpu_custom_call" | custom-call | tf_op jit(solution)/shard_map/weights/pallas_call | solution.py:289
  60.7 7.3 %all-to-all-done.2 = bf16[32,8,512]{2,1,0:T(8,128)(2,1)S(1)} async-done(((bf16[32,8,512]{2,1,0:T(8,128)(2,1)}), bf16[32,8,512]{2,1,0:T(8,128)(2,1)S(1)}, u32[]{:S(2)}, u32[]{:S(2)}) %all-to-all-start.2) | async-done | bytes 262176 | tf_op jit(solution)/shard_map/all_to_all | solution.py:325
  67.9 0.0 copy-done.3
  67.9 1.6 %degrid.1 = (f32[4,128]{1,0:T(4,128)}, f32[4,128]{1,0:T(4,128)}) custom-call(s32[4]{0:T(128)S(1)} %bitcast.14, bf16[256,512]{1,0:T(8,128)(2,1)S(1)} %bitcast.10, bf16[256,512]{1,0:T(8,128)(2,1)S(1)} %get-tuple-element.7.row_ref, bf16[256,512]{1,0:T(8,128)(2,1)S(1)} %get-tuple-element.8.high_ref, bf16[256,512]{1,0:T(8,128)(2,1)S(1)} %get-tuple-element.9.low_ref), custom_call_target="tpu_custom_call" | custom-call | tf_op jit(solution)/shard_map/degrid/pallas_call | solution.py:314
Async XLA Ops:
  0.6 24.2 %copy-start.2 = (s32[16]{0:T(128)S(1)}, s32[16]{0:T(128)}, u32[]{:S(2)}) copy-start(s32[16]{0:T(128)} %sub_ref.1) | copy-start | bytes 196
  5.3 19.5 %all-to-all-start = ((bf16[32,32,128]{2,1,0:T(8,128)(2,1)}), bf16[32,32,128]{2,1,0:T(8,128)(2,1)S(1)}, u32[]{:S(2)}, u32[]{:S(2)}) async-start(bf16[32,32,128]{2,1,0:T(8,128)(2,1)} %first_axis.1), calls=%async_computation | async-start | bytes 524288 | tf_op jit(solution)/shard_map/all_to_all | solution.py:325
  16.8 42.1 %copy-start.4 = (f32[16,8]{0,1:T(8,128)S(1)}, f32[16,8]{0,1:T(8,128)}, u32[]{:S(2)}) copy-start(f32[16,8]{0,1:T(8,128)} %param.12) | copy-start | bytes 1540
  16.8 42.1 %copy-start = (s32[2,1,4,128]{3,2,1,0:T(4,128)S(1)}, s32[2,1,4,128]{3,2,1,0:T(4,128)}, u32[]{:S(2)}) copy-start(s32[2,1,4,128]{3,2,1,0:T(4,128)} %param.14) | copy-start | bytes 12292
  16.9 42.1 %copy-start.1 = (s32[2,1,4,128]{3,2,1,0:T(4,128)S(1)}, s32[2,1,4,128]{3,2,1,0:T(4,128)}, u32[]{:S(2)}) copy-start(s32[2,1,4,128]{3,2,1,0:T(4,128)} %param.15) | copy-start | bytes 12292
  16.9 51.1 %copy-start.3 = (s32[1,4]{1,0:T(1,128)S(1)}, s32[1,4]{1,0:T(1,128)}, u32[]{:S(2)}) copy-start(s32[1,4]{1,0:T(1,128)} %param.13) | copy-start | bytes 52
  52.5 15.4 %all-to-all-start.2 = ((bf16[32,8,512]{2,1,0:T(8,128)(2,1)}), bf16[32,8,512]{2,1,0:T(8,128)(2,1)S(1)}, u32[]{:S(2)}, u32[]{:S(2)}) async-start(bf16[32,8,512]{2,1,0:T(8,128)(2,1)} %own_rows.1), calls=%async_computation.2 | async-start | bytes 524288 | tf_op jit(solution)/shard_map/all_to_all | solution.py:325

commit v3 on v2

--- a/solution.py
+++ b/solution.py
@@ -13,7 +13,7 @@
 LANES = 128
 PAIRS = 4
 LOADS = 4
-READY = 3072
+READY = 2304
 PARAMS = pltpu.CompilerParams(vmem_limit_bytes=16 * 1024 * 1024)
 MIDDLE = pltpu.CompilerParams(vmem_limit_bytes=24 * 1024 * 1024)
 WIDE = pltpu.CompilerParams(vmem_limit_bytes=60 * 1024 * 1024)
@@ -262,7 +262,7 @@
     )(terms)
 
 
-def weights_kernel(kernel_ref, cell_ref, frac_ref, row_ref, high_ref, low_ref):
+def weights_kernel(kernel_ref, cell_ref, frac_ref, row_ref, col_ref):
     blocks, slots = cell_ref.shape[1:]
     for b in range(blocks):
         lanes = slice(b * slots, (b + 1) * slots)
@@ -279,46 +279,44 @@
                 row_ref[:, lanes] = spread.astype(bf16)
             else:
                 high = spread.astype(bf16)
-                high_ref[:, lanes] = high
-                low_ref[:, lanes] = (spread - high.astype(f32)).astype(bf16)
+                col_ref[:S, lanes] = high
+                col_ref[S:, lanes] = (spread - high.astype(f32)).astype(bf16)
 
 
 def weights(kernel, cells, fracs):
     total = cells.shape[1] * cells.shape[2]
-    shape = jax.ShapeDtypeStruct((S, total), bf16)
     return pl.pallas_call(
         weights_kernel,
         in_specs=[SMEM, VMEM, VMEM],
-        out_specs=[VMEM] * 3,
-        out_shape=[shape] * 3,
+        out_specs=[VMEM] * 2,
+        out_shape=[jax.ShapeDtypeStruct((S, total), bf16), jax.ShapeDtypeStruct((2 * S, total), bf16)],
         compiler_params=PARAMS,
         name="weights",
     )(kernel, cells, fracs)
 
 
-def degrid_kernel(count_ref, grid_ref, row_ref, high_ref, low_ref, re_ref, im_ref):
+def degrid_kernel(count_ref, grid_ref, row_ref, col_ref, re_ref, im_ref):
     blocks, slots = re_ref.shape
     row = row_ref[...].astype(f32)
+    cells = jnp.concatenate([grid_ref[:, :S], grid_ref[:, S:]], axis=0)
+    sums = jnp.dot(jnp.concatenate([cells, cells], axis=1), col_ref[...], preferred_element_type=f32)
     for part, out_ref in ((0, re_ref), (1, im_ref)):
-        cells = grid_ref[:, part * S : (part + 1) * S]
-        sums = jnp.dot(cells, high_ref[...], preferred_element_type=f32)
-        sums = sums + jnp.dot(cells, low_ref[...], preferred_element_type=f32)
-        values = jnp.sum(sums * row, axis=0, keepdims=True)
+        values = jnp.sum(sums[part * S : (part + 1) * S] * row, axis=0, keepdims=True)
         for b in range(blocks):
             live = lax.broadcasted_iota(jnp.int32, (1, slots), 1) < count_ref[b]
             out_ref[b : b + 1, :] = jnp.where(live, values[:, b * slots : (b + 1) * slots], 0.0)
 
 
-def degrid(counts, grid, row, high, low, blocks, slots):
+def degrid(counts, grid, row, col, blocks, slots):
     shape = jax.ShapeDtypeStruct((blocks, slots), f32)
     return pl.pallas_call(
         degrid_kernel,
-        in_specs=[SMEM] + [VMEM] * 4,
+        in_specs=[SMEM] + [VMEM] * 3,
         out_specs=[VMEM] * 2,
         out_shape=[shape] * 2,
         compiler_params=PARAMS,
         name="degrid",
-    )(counts, grid, row, high, low)
+    )(counts, grid, row, col)
 
 
 def exchange(x, axis):
@@ -332,11 +330,12 @@
     blocks, slots = cell_index.shape[2:]
     band = exchange(first_axis(col_offsets, sky_re[0], sky_im[0]), "col")
     start = (lax.axis_index("facet") * pixels).astype(jnp.int32).reshape(1)
+    row, column = weights(kernel, cell_index[:, 0], frac_index[:, 0])
+    band, row, column = lax.optimization_barrier((band, row, column))
     terms = second_axis(start, sub_offsets, band, second_table(start, READY))
     arrived = exchange(terms.reshape(n_sub, 8, 2 * S), "facet")
-    row, high, low = weights(kernel, cell_index[:, 0], frac_index[:, 0])
     grid = exchange(own_rows(arrived, col), "col").reshape(S, 2 * S)
-    vis_re, vis_im = degrid(vis_count[0], grid, row, high, low, blocks, slots)
+    vis_re, vis_im = degrid(vis_count[0], grid, row, column, blocks, slots)
     return vis_re[None], vis_im[None]
 
 

time: 69.8 us -> 68.9 us (0.987)
  blocking collectives: 24.9 us -> 40.1 us
  waiting for transfers between devices: 15.2 us -> 6.47 us
  starting transfers between devices: 16.8 us -> 10.4 us
  Pallas kernels: 11.7 us -> 10.8 us
    all_to_all x1 -> x2, blocking collectives: 24.9 us -> 40.1 us  [exchange(): return lax.all_to_all(x, axis, split_axis=0, concat_axis=0, tiled=True)]
    all_to_all x2 -> x1, waiting for transfers between devices: 15.2 us -> 6.47 us  [exchange(): return lax.all_to_all(x, axis, split_axis=0, concat_axis=0, tiled=True)]
    all_to_all x2 -> x1, starting transfers between devices: 16.8 us -> 10.4 us  [exchange(): return lax.all_to_all(x, axis, split_axis=0, concat_axis=0, tiled=True)]
    pallas_call x1, Pallas kernels: 0.75 us -> 0.04 us  [own_rows(): pl.pallas_call(own_rows_kernel, in_specs=[VMEM], out_specs=VMEM, out_shap...]
  transfers between devices with their start and end apart: 2 -> 1, of which waited for: 2 -> 1; matrix products, arithmetic and copies ran while one was open for 0% -> 0% of each run, Pallas kernels for 4% -> 4%
where the time goes in v3:
time: 68.9 us; the launch traced here: 68.7 us
  blocking collectives  40.1 us (58%)
  Pallas kernels  10.8 us (16%)
  starting transfers between devices  10.4 us (15%)
  waiting for transfers between devices  6.47 us (9%)
  between operations  0.74 us (1%)
    all_to_all x2, blocking collectives, exchange(): return lax.all_to_all(x, axis, split_axis=0, concat_axis=0, tiled=True)  40.1 us
    all_to_all x1, starting transfers between devices, exchange(): return lax.all_to_all(x, axis, split_axis=0, concat_axis=0, tiled=True)  10.4 us
    all_to_all x1, waiting for transfers between devices, exchange(): return lax.all_to_all(x, axis, split_axis=0, concat_axis=0, tiled=True)  6.47 us
    pallas_call x1, Pallas kernels, first_axis(): pl.pallas_call(first_axis_kernel, in_specs=[HBM] * 3, out_specs=VMEM, out...  4.66 us
    pallas_call x1, Pallas kernels, second_axis(): pl.pallas_call(second_axis_kernel, in_specs=[SMEM, SMEM, VMEM, VMEM], out...  2.06 us
    pallas_call x1, Pallas kernels, weights(): pl.pallas_call(weights_kernel, in_specs=[SMEM, VMEM, VMEM], out_specs=[VM...  1.68 us
    pallas_call x1, Pallas kernels, degrid(): pl.pallas_call(degrid_kernel, in_specs=[SMEM] + [VMEM] * 3, out_specs=[VM...  1.57 us
  transfers between devices with their start and end apart: 1, of which 1 were waited for; matrix products, arithmetic and copies ran while one was open for 0% of the time, Pallas kernels for 4%

profile of v3, /device:TPU:1, one launch (start us, length us, event | category | flops | bytes accessed | tf_op | source)
XLA Modules:
  0.0 68.7 jit_solution(17931866687373360320)
XLA Ops:
  0.6 0.0 copy-start.4
  0.6 0.0 copy-start
  0.7 0.0 copy-start.1
  0.7 0.0 copy-start.2
  0.7 4.7 %first_axis.1 = bf16[32,32,128]{2,1,0:T(8,128)(2,1)} custom-call(s32[2]{0:T(128)} %col_hbm.1, bf16[4096,128]{1,0:T(8,128)(2,1)} %bitcast.15, bf16[4096,128]{1,0:T(8,128)(2,1)} %bitcast.16), custom_call_target="tpu_custom_call" | custom-call | tf_op jit(solution)/shard_map/first_axis/pallas_call | solution.py:120
  5.3 10.4 %all-to-all-start = ((bf16[32,32,128]{2,1,0:T(8,128)(2,1)}), bf16[32,32,128]{2,1,0:T(8,128)(2,1)S(1)}, u32[]{:S(2)}, u32[]{:S(2)}) async-start(bf16[32,32,128]{2,1,0:T(8,128)(2,1)} %first_axis.1), calls=%async_computation | async-start | bytes 524288 | tf_op jit(solution)/shard_map/all_to_all | solution.py:323
  15.8 0.0 copy-done.4
  15.8 0.1 copy.10.kernel_ref
  15.8 0.8 %second_table.1.ready_ref = bf16[2304,512]{1,0:T(8,128)(2,1)S(1)} custom-call(s32[1]{0:T(128)} %bitcast.1.start_ref), custom_call_target="tpu_custom_call" | custom-call | tf_op jit(solution)/shard_map/second_table/pallas_call | solution.py:171
  16.7 0.0 copy-start.3
  16.7 0.0 copy-done
  16.7 0.0 copy-done.1
  16.7 1.7 %weights.1 = (bf16[256,512]{1,0:T(8,128)(2,1)S(1)}, bf16[512,512]{1,0:T(8,128)(2,1)S(1)}) custom-call(f32[16,8]{1,0:T(8,128)S(1)} %copy.10.kernel_ref, s32[2,4,128]{2,1,0:T(4,128)S(1)} %bitcast.12, s32[2,4,128]{2,1,0:T(4,128)S(1)} %bitcast.13), custom_call_target="tpu_custom_call" | custom-call | tf_op jit(solution)/shard_map/weights/pallas_call | solution.py:288
  18.4 6.5 %all-to-all-done.band_ref = bf16[32,32,128]{2,1,0:T(8,128)(2,1)S(1)} async-done(((bf16[32,32,128]{2,1,0:T(8,128)(2,1)}), bf16[32,32,128]{2,1,0:T(8,128)(2,1)S(1)}, u32[]{:S(2)}, u32[]{:S(2)}) %all-to-all-start) | async-done | bytes 262176 | tf_op jit(solution)/shard_map/all_to_all | solution.py:323
  24.9 0.0 copy-done.2
  24.9 2.1 %second_axis.1 = bf16[128,512]{1,0:T(8,128)(2,1)S(1)} custom-call(s32[1]{0:T(128)} %bitcast.1.start_ref, s32[16]{0:T(128)S(1)} %copy-done.2, bf16[32,32,128]{2,1,0:T(8,128)(2,1)S(1)} %all-to-all-done.band_ref, bf16[2304,512]{1,0:T(8,128)(2,1)S(1)} %second_table.1.ready_ref), custom_call_target="tpu_custom_call" | custom-call | tf_op jit(solution)/shard_map/second_axis/pallas_call | solution.py:230
  26.9 24.9 %all_to_all.15.terms_ref = bf16[16,8,512]{2,1,0:T(8,128)(2,1)S(1)} all-to-all(bf16[16,8,512]{2,1,0:T(8,128)(2,1)S(1)} %bitcast.11), channel_id=1, replica_groups=mesh['facet'=16,'col'=32] {'facet'}, dimensions={0} | all-to-all | bytes 262144 | tf_op jit(solution)/shard_map/all_to_all | solution.py:323
  51.9 15.2 %all_to_all.16 = bf16[32,8,512]{2,1,0:T(8,128)(2,1)S(1)} all-to-all(bf16[32,8,512]{2,1,0:T(8,128)(2,1)S(1)} %own_rows.1), channel_id=1, replica_groups=mesh['facet'=16,'col'=32] {'col'}, dimensions={0} | all-to-all | bytes 524288 | tf_op jit(solution)/shard_map/all_to_all | solution.py:323
  67.1 0.0 copy-done.3
  67.1 1.6 %degrid.1 = (f32[4,128]{1,0:T(4,128)}, f32[4,128]{1,0:T(4,128)}) custom-call(s32[4]{0:T(128)S(1)} %bitcast.14, bf16[256,512]{1,0:T(8,128)(2,1)S(1)} %bitcast.10, bf16[256,512]{1,0:T(8,128)(2,1)S(1)} %get-tuple-element.12.row_ref, bf16[512,512]{1,0:T(8,128)(2,1)S(1)} %get-tuple-element.13.col_ref), custom_call_target="tpu_custom_call" | custom-call | tf_op jit(solution)/shard_map/degrid/pallas_call | solution.py:312
  (1 shorter events, 0.0 us)
Async XLA Ops:
  0.6 15.1 %copy-start.4 = (f32[16,8]{0,1:T(8,128)S(1)}, f32[16,8]{0,1:T(8,128)}, u32[]{:S(2)}) copy-start(f32[16,8]{0,1:T(8,128)} %param.12) | copy-start | bytes 1540
  0.6 16.0 %copy-start = (s32[2,1,4,128]{3,2,1,0:T(4,128)S(1)}, s32[2,1,4,128]{3,2,1,0:T(4,128)}, u32[]{:S(2)}) copy-start(s32[2,1,4,128]{3,2,1,0:T(4,128)} %param.14) | copy-start | bytes 12292
  0.7 16.0 %copy-start.1 = (s32[2,1,4,128]{3,2,1,0:T(4,128)S(1)}, s32[2,1,4,128]{3,2,1,0:T(4,128)}, u32[]{:S(2)}) copy-start(s32[2,1,4,128]{3,2,1,0:T(4,128)} %param.15) | copy-start | bytes 12292
  0.7 24.2 %copy-start.2 = (s32[16]{0:T(128)S(1)}, s32[16]{0:T(128)}, u32[]{:S(2)}) copy-start(s32[16]{0:T(128)} %sub_ref.1) | copy-start | bytes 196
  5.3 19.5 %all-to-all-start = ((bf16[32,32,128]{2,1,0:T(8,128)(2,1)}), bf16[32,32,128]{2,1,0:T(8,128)(2,1)S(1)}, u32[]{:S(2)}, u32[]{:S(2)}) async-start(bf16[32,32,128]{2,1,0:T(8,128)(2,1)} %first_axis.1), calls=%async_computation | async-start | bytes 524288 | tf_op jit(solution)/shard_map/all_to_all | solution.py:323
  16.7 50.4 %copy-start.3 = (s32[1,4]{1,0:T(1,128)S(1)}, s32[1,4]{1,0:T(1,128)}, u32[]{:S(2)}) copy-start(s32[1,4]{1,0:T(1,128)} %param.13) | copy-start | bytes 52

commit v4 on v3

--- a/solution.py
+++ b/solution.py
@@ -134,24 +134,26 @@
     )(col_offsets, sky_re, sky_im)
 
 
-def table_blocks(start, step_ref, blocks):
+def table_parts(start, parts_ref):
     cells = lax.broadcasted_iota(jnp.int32, (8, S), 1)
     row = lax.broadcasted_iota(jnp.int32, (8, S), 0)
+    for i, mult in enumerate((8 * row, 8 * row + 64, 8 * row + 128, row + 128)):
+        scale = 1.0 / 256 if i == 3 else 1.0
+        for k, phase in enumerate(cos_sin(mult * cells)):
+            parts_ref[k, 8 * i : 8 * i + 8, :] = phase * scale
     for i in range(2):
-        c, s = cos_sin((row + 8 * i) * 8 * cells)
-        step_ref[0, 8 * i : 8 * i + 8, :] = c
-        step_ref[1, 8 * i : 8 * i + 8, :] = s
-    last = cos_sin(cells[:1] * 128)
-    base_c, base_s = cos_sin((row + 128) * cells)
-    base_c, base_s = base_c * (1.0 / 256), base_s * (1.0 / 256)
-    block = lax.broadcasted_iota(jnp.int32, (16, S), 0)
-    block_c, block_s = cos_sin((start + 256 * block) * lax.broadcasted_iota(jnp.int32, (16, S), 1))
+        for k, phase in enumerate(cos_sin((start + 256 * (8 * i + row)) * cells)):
+            parts_ref[k, 32 + 8 * i : 40 + 8 * i, :] = phase
+
+
+def table_blocks(parts_ref, blocks):
     made = []
     for g in blocks:
-        bc, bs = cmul(base_c, base_s, block_c[g : g + 1], block_s[g : g + 1])
+        block = slice(32 + g, 33 + g)
+        bc, bs = cmul(parts_ref[0, 24:32], parts_ref[1, 24:32], parts_ref[0, block], parts_ref[1, block])
         up, down = [], []
         for d in range(1, 17):
-            hc, hs = last if d == 16 else (step_ref[0, d : d + 1, :], step_ref[1, d : d + 1, :])
+            hc, hs = parts_ref[0, d : d + 1], parts_ref[1, d : d + 1]
             cc, ss, sc, cs = bc * hc, bs * hs, bs * hc, bc * hs
             if d < 16:
                 up.append(jnp.concatenate([cc - ss, sc + cs], axis=1))
@@ -161,43 +163,49 @@
     return made
 
 
-def second_table_kernel(start_ref, table_ref, step_ref):
+def second_table_kernel(start_ref, sub_ref, table_ref, parts_ref, phases_ref):
+    start = start_ref[0]
+    table_parts(start, parts_ref)
     blocks = range(table_ref.shape[0] // 256)
-    for g, made in zip(blocks, table_blocks(start_ref[0], step_ref, blocks)):
+    for g, made in zip(blocks, table_blocks(parts_ref, blocks)):
         table_ref[g * 256 : (g + 1) * 256, :] = made
-
-
-def second_table(start, rows):
-    return pl.pallas_call(
-        second_table_kernel,
-        in_specs=[SMEM],
-        out_specs=VMEM,
-        out_shape=jax.ShapeDtypeStruct((rows, 2 * S), bf16),
-        scratch_shapes=[pltpu.VMEM((2, 16, S), f32)],
-        compiler_params=PARAMS,
-        name="second_table",
-    )(start)
-
-
-def second_axis_kernel(start_ref, sub_ref, band_ref, ready_ref, out_ref, shift_ref, table_ref, step_ref):
     n_sub = sub_ref.shape[0]
-    chunks = band_ref.shape[0]
-    per = n_sub // SCOL
-    start = start_ref[0]
-    ready = ready_ref.shape[0]
     row = lax.broadcasted_iota(jnp.int32, (n_sub, LANES), 0)
     lane = lax.broadcasted_iota(jnp.int32, (n_sub, LANES), 1)
     offs = jnp.zeros((n_sub, LANES), jnp.int32)
     for s in range(n_sub):
         offs = jnp.where(row == s, sub_ref[s], offs)
-    low_c, low_s = cos_sin(offs * lane)
-    high_c, high_s = cos_sin(offs * (lane * LANES + start))
+    phases_ref[0], phases_ref[1] = cos_sin(offs * lane)
+    phases_ref[2], phases_ref[3] = cos_sin(offs * (lane * LANES + start))
+
+
+def second_table(start, sub_offsets, rows):
+    return pl.pallas_call(
+        second_table_kernel,
+        in_specs=[SMEM, SMEM],
+        out_specs=[VMEM] * 3,
+        out_shape=[
+            jax.ShapeDtypeStruct((rows, 2 * S), bf16),
+            jax.ShapeDtypeStruct((2, 48, S), f32),
+            jax.ShapeDtypeStruct((4, sub_offsets.shape[0], LANES), f32),
+        ],
+        compiler_params=PARAMS,
+        name="second_table",
+    )(start, sub_offsets)
+
+
+def second_axis_kernel(band_ref, ready_ref, parts_ref, phases_ref, out_ref, shift_ref, table_ref):
+    n_sub = phases_ref.shape[1]
+    chunks = band_ref.shape[0]
+    per = n_sub // SCOL
+    ready = ready_ref.shape[0]
+    low_c, low_s, high_c, high_s = (phases_ref[i] for i in range(4))
     for b in range(chunks):
         lanes = slice(b * LANES, (b + 1) * LANES)
         c, d = cmul(low_c, low_s, high_c[:, b : b + 1], high_s[:, b : b + 1])
         shift_ref[0, :, lanes] = c
         shift_ref[1, :, lanes] = d
-    for g, made in enumerate(table_blocks(start, step_ref, range(ready // 256, chunks // 2))):
+    for g, made in enumerate(table_blocks(parts_ref, range(ready // 256, chunks // 2))):
         table_ref[g * 256 : (g + 1) * 256, :] = made
 
     def shifted(q):
@@ -224,22 +232,21 @@
     out_ref[:, S:] = im.reshape(n_sub * 8, S).astype(bf16)
 
 
-def second_axis(start, sub_offsets, band, ready):
-    n_sub = sub_offsets.shape[0]
+def second_axis(band, ready, parts, phases):
+    n_sub = phases.shape[1]
     pixels = band.shape[0] * LANES
     return pl.pallas_call(
         second_axis_kernel,
-        in_specs=[SMEM, SMEM, VMEM, VMEM],
+        in_specs=[VMEM] * 4,
         out_specs=VMEM,
         out_shape=jax.ShapeDtypeStruct((n_sub * 8, 2 * S), bf16),
         scratch_shapes=[
             pltpu.VMEM((2, n_sub, pixels), f32),
             pltpu.VMEM((pixels - ready.shape[0], 2 * S), bf16),
-            pltpu.VMEM((2, 16, S), f32),
         ],
         compiler_params=MIDDLE,
         name="second_axis",
-    )(start, sub_offsets, band, ready)
+    )(band, ready, parts, phases)
 
 
 def own_rows_kernel(terms_ref, out_ref):
@@ -262,7 +269,7 @@
     )(terms)
 
 
-def weights_kernel(kernel_ref, cell_ref, frac_ref, row_ref, col_ref):
+def weights_kernel(count_ref, kernel_ref, cell_ref, frac_ref, row_ref, col_ref):
     blocks, slots = cell_ref.shape[1:]
     for b in range(blocks):
         lanes = slice(b * slots, (b + 1) * slots)
@@ -276,26 +283,27 @@
                     tap = jnp.where(frac == o, kernel_ref[o, a], tap)
                 spread = jnp.where(ahead == a, tap, spread)
             if axis == 0:
-                row_ref[:, lanes] = spread.astype(bf16)
+                live = lax.broadcasted_iota(jnp.int32, (1, slots), 1) < count_ref[b]
+                row_ref[:, lanes] = jnp.where(live, spread, 0.0).astype(bf16)
             else:
                 high = spread.astype(bf16)
                 col_ref[:S, lanes] = high
                 col_ref[S:, lanes] = (spread - high.astype(f32)).astype(bf16)
 
 
-def weights(kernel, cells, fracs):
+def weights(counts, kernel, cells, fracs):
     total = cells.shape[1] * cells.shape[2]
     return pl.pallas_call(
         weights_kernel,
-        in_specs=[SMEM, VMEM, VMEM],
+        in_specs=[SMEM, SMEM, VMEM, VMEM],
         out_specs=[VMEM] * 2,
         out_shape=[jax.ShapeDtypeStruct((S, total), bf16), jax.ShapeDtypeStruct((2 * S, total), bf16)],
         compiler_params=PARAMS,
         name="weights",
-    )(kernel, cells, fracs)
-
-
-def degrid_kernel(count_ref, grid_ref, row_ref, col_ref, re_ref, im_ref):
+    )(counts, kernel, cells, fracs)
+
+
+def degrid_kernel(grid_ref, row_ref, col_ref, re_ref, im_ref):
     blocks, slots = re_ref.shape
     row = row_ref[...].astype(f32)
     cells = jnp.concatenate([grid_ref[:, :S], grid_ref[:, S:]], axis=0)
@@ -303,20 +311,19 @@
     for part, out_ref in ((0, re_ref), (1, im_ref)):
         values = jnp.sum(sums[part * S : (part + 1) * S] * row, axis=0, keepdims=True)
         for b in range(blocks):
-            live = lax.broadcasted_iota(jnp.int32, (1, slots), 1) < count_ref[b]
-            out_ref[b : b + 1, :] = jnp.where(live, values[:, b * slots : (b + 1) * slots], 0.0)
-
-
-def degrid(counts, grid, row, col, blocks, slots):
+            out_ref[b : b + 1, :] = values[:, b * slots : (b + 1) * slots]
+
+
+def degrid(grid, row, col, blocks, slots):
     shape = jax.ShapeDtypeStruct((blocks, slots), f32)
     return pl.pallas_call(
         degrid_kernel,
-        in_specs=[SMEM] + [VMEM] * 3,
+        in_specs=[VMEM] * 3,
         out_specs=[VMEM] * 2,
         out_shape=[shape] * 2,
         compiler_params=PARAMS,
         name="degrid",
-    )(counts, grid, row, col)
+    )(grid, row, col)
 
 
 def exchange(x, axis):
@@ -330,12 +337,12 @@
     blocks, slots = cell_index.shape[2:]
     band = exchange(first_axis(col_offsets, sky_re[0], sky_im[0]), "col")
     start = (lax.axis_index("facet") * pixels).astype(jnp.int32).reshape(1)
-    row, column = weights(kernel, cell_index[:, 0], frac_index[:, 0])
+    row, column = weights(vis_count[0], kernel, cell_index[:, 0], frac_index[:, 0])
     band, row, column = lax.optimization_barrier((band, row, column))
-    terms = second_axis(start, sub_offsets, band, second_table(start, READY))
+    terms = second_axis(band, *second_table(start, sub_offsets, READY))
     arrived = exchange(terms.reshape(n_sub, 8, 2 * S), "facet")
     grid = exchange(own_rows(arrived, col), "col").reshape(S, 2 * S)
-    vis_re, vis_im = degrid(vis_count[0], grid, row, column, blocks, slots)
+    vis_re, vis_im = degrid(grid, row, column, blocks, slots)
     return vis_re[None], vis_im[None]
 
 

time: 68.9 us -> 67.8 us (0.984)
  waiting for transfers between devices: 6.47 us -> 5.2 us
    all_to_all x1, waiting for transfers between devices: 6.47 us -> 5.2 us  [exchange(): return lax.all_to_all(x, axis, split_axis=0, concat_axis=0, tiled=True)]
  transfers between devices with their start and end apart: 1 -> 1, of which waited for: 1 -> 1; matrix products, arithmetic and copies ran while one was open for 0% -> 0% of each run, Pallas kernels for 4% -> 5%
where the time goes in v4:
time: 67.8 us; the launch traced here: 67.5 us
  blocking collectives  40.1 us (59%)
  starting transfers between devices  10.4 us (15%)
  Pallas kernels  10.3 us (15%)
  waiting for transfers between devices  5.2 us (8%)
  local copies, waits for them, and re-layouts  0.74 us (1%)
  between operations  0.74 us (1%)
    all_to_all x2, blocking collectives, exchange(): return lax.all_to_all(x, axis, split_axis=0, concat_axis=0, tiled=True)  40.1 us
    all_to_all x1, starting transfers between devices, exchange(): return lax.all_to_all(x, axis, split_axis=0, concat_axis=0, tiled=True)  10.4 us
    all_to_all x1, waiting for transfers between devices, exchange(): return lax.all_to_all(x, axis, split_axis=0, concat_axis=0, tiled=True)  5.2 us
    pallas_call x1, Pallas kernels, first_axis(): pl.pallas_call(first_axis_kernel, in_specs=[HBM] * 3, out_specs=VMEM, out...  4.66 us
    pallas_call x1, Pallas kernels, weights(): pl.pallas_call(weights_kernel, in_specs=[SMEM, SMEM, VMEM, VMEM], out_spe...  1.7 us
    pallas_call x1, Pallas kernels, second_axis(): pl.pallas_call(second_axis_kernel, in_specs=[VMEM] * 4, out_specs=VMEM, o...  1.46 us
    pallas_call x1, Pallas kernels, second_table(): pl.pallas_call(second_table_kernel, in_specs=[SMEM, SMEM], out_specs=[VME...  1.43 us
  transfers between devices with their start and end apart: 1, of which 1 were waited for; matrix products, arithmetic and copies ran while one was open for 0% of the time, Pallas kernels for 5%

profile of v4, /device:TPU:1, one launch (start us, length us, event | category | flops | bytes accessed | tf_op | source)
XLA Modules:
  0.0 67.5 jit_solution(6453521134400700258)
XLA Ops:
  0.6 0.0 copy-start.4
  0.6 0.0 copy-start.3
  0.7 0.0 copy-start.1
  0.7 0.0 copy-start
  0.7 4.7 %first_axis.1 = bf16[32,32,128]{2,1,0:T(8,128)(2,1)} custom-call(s32[2]{0:T(128)} %col_hbm.1, bf16[4096,128]{1,0:T(8,128)(2,1)} %bitcast.15, bf16[4096,128]{1,0:T(8,128)(2,1)} %bitcast.16), custom_call_target="tpu_custom_call" | custom-call | tf_op jit(solution)/shard_map/first_axis/pallas_call | solution.py:120
  5.3 10.4 %all-to-all-start = ((bf16[32,32,128]{2,1,0:T(8,128)(2,1)}), bf16[32,32,128]{2,1,0:T(8,128)(2,1)S(1)}, u32[]{:S(2)}, u32[]{:S(2)}) async-start(bf16[32,32,128]{2,1,0:T(8,128)(2,1)} %first_axis.1), calls=%async_computation | async-start | bytes 524288 | tf_op jit(solution)/shard_map/all_to_all | solution.py:330
  15.8 0.0 copy-done.4
  15.8 0.1 copy.10.kernel_ref
  15.8 0.0 copy-done.3
  15.8 1.4 %second_table.1 = (bf16[2304,512]{1,0:T(8,128)(2,1)S(1)}, f32[2,48,256]{2,1,0:T(8,128)S(1)}, f32[4,16,128]{2,1,0:T(8,128)S(1)}) custom-call(s32[1]{0:T(128)} %bitcast.5.start_ref, s32[16]{0:T(128)S(1)} %copy-done.3), custom_call_target="tpu_custom_call" | custom-call | tf_op jit(solution)/shard_map/second_table/pallas_call | solution.py:183
  17.3 0.0 copy-done.1
  17.3 0.0 copy-done
  17.3 0.0 copy-start.2
  17.3 0.6 copy-done.2
  18.0 1.7 %weights.1 = (bf16[256,512]{1,0:T(8,128)(2,1)S(1)}, bf16[512,512]{1,0:T(8,128)(2,1)S(1)}) custom-call(s32[4]{0:T(128)S(1)} %bitcast.14, f32[16,8]{1,0:T(8,128)S(1)} %copy.10.kernel_ref, s32[2,4,128]{2,1,0:T(4,128)S(1)} %bitcast.12, s32[2,4,128]{2,1,0:T(4,128)S(1)} %bitcast.13), custom_call_target="tpu_custom_call" | custom-call | tf_op jit(solution)/shard_map/weights/pallas_call | solution.py:296
  19.7 5.2 %all-to-all-done.band_ref = bf16[32,32,128]{2,1,0:T(8,128)(2,1)S(1)} async-done(((bf16[32,32,128]{2,1,0:T(8,128)(2,1)}), bf16[32,32,128]{2,1,0:T(8,128)(2,1)S(1)}, u32[]{:S(2)}, u32[]{:S(2)}) %all-to-all-start) | async-done | bytes 262176 | tf_op jit(solution)/shard_map/all_to_all | solution.py:330
  24.9 1.5 %second_axis.1 = bf16[128,512]{1,0:T(8,128)(2,1)S(1)} custom-call(bf16[32,32,128]{2,1,0:T(8,128)(2,1)S(1)} %all-to-all-done.band_ref, bf16[2304,512]{1,0:T(8,128)(2,1)S(1)} %get-tuple-element.15.ready_ref, f32[2,48,256]{2,1,0:T(8,128)S(1)} %get-tuple-element.16.parts_ref, f32[4,16,128]{2,1,0:T(8,128)S(1)} %get-tuple-element.17.phases_ref), custom_call_target="tpu_custom_call" | custom-call | tf_op jit(solution)/shard_map/second_axis/pallas_call | solution.py:238
  26.3 24.9 %all_to_all.15.terms_ref = bf16[16,8,512]{2,1,0:T(8,128)(2,1)S(1)} all-to-all(bf16[16,8,512]{2,1,0:T(8,128)(2,1)S(1)} %bitcast.11), channel_id=1, replica_groups=mesh['facet'=16,'col'=32] {'facet'}, dimensions={0} | all-to-all | bytes 262144 | tf_op jit(solution)/shard_map/all_to_all | solution.py:330
  51.3 15.1 %all_to_all.16 = bf16[32,8,512]{2,1,0:T(8,128)(2,1)S(1)} all-to-all(bf16[32,8,512]{2,1,0:T(8,128)(2,1)S(1)} %own_rows.1), channel_id=1, replica_groups=mesh['facet'=16,'col'=32] {'col'}, dimensions={0} | all-to-all | bytes 524288 | tf_op jit(solution)/shard_map/all_to_all | solution.py:330
  66.5 1.0 %degrid.1 = (f32[4,128]{1,0:T(4,128)}, f32[4,128]{1,0:T(4,128)}) custom-call(bf16[256,512]{1,0:T(8,128)(2,1)S(1)} %bitcast.10, bf16[256,512]{1,0:T(8,128)(2,1)S(1)} %get-tuple-element.18.row_ref, bf16[512,512]{1,0:T(8,128)(2,1)S(1)} %get-tuple-element.19.col_ref), custom_call_target="tpu_custom_call" | custom-call | tf_op jit(solution)/shard_map/degrid/pallas_call | solution.py:319
  (1 shorter events, 0.0 us)
Async XLA Ops:
  0.6 15.1 %copy-start.4 = (f32[16,8]{0,1:T(8,128)S(1)}, f32[16,8]{0,1:T(8,128)}, u32[]{:S(2)}) copy-start(f32[16,8]{0,1:T(8,128)} %param.12) | copy-start | bytes 1540
  0.6 15.2 %copy-start.3 = (s32[16]{0:T(128)S(1)}, s32[16]{0:T(128)}, u32[]{:S(2)}) copy-start(s32[16]{0:T(128)} %sub_ref.1) | copy-start | bytes 196
  0.7 16.6 %copy-start.1 = (s32[2,1,4,128]{3,2,1,0:T(4,128)S(1)}, s32[2,1,4,128]{3,2,1,0:T(4,128)}, u32[]{:S(2)}) copy-start(s32[2,1,4,128]{3,2,1,0:T(4,128)} %param.15) | copy-start | bytes 12292
  0.7 16.6 %copy-start = (s32[2,1,4,128]{3,2,1,0:T(4,128)S(1)}, s32[2,1,4,128]{3,2,1,0:T(4,128)}, u32[]{:S(2)}) copy-start(s32[2,1,4,128]{3,2,1,0:T(4,128)} %param.14) | copy-start | bytes 12292
  5.3 19.5 %all-to-all-start = ((bf16[32,32,128]{2,1,0:T(8,128)(2,1)}), bf16[32,32,128]{2,1,0:T(8,128)(2,1)S(1)}, u32[]{:S(2)}, u32[]{:S(2)}) async-start(bf16[32,32,128]{2,1,0:T(8,128)(2,1)} %first_axis.1), calls=%async_computation | async-start | bytes 524288 | tf_op jit(solution)/shard_map/all_to_all | solution.py:330
  17.3 0.7 copy-start.2

commit v5 on v4

--- a/solution.py
+++ b/solution.py
@@ -12,7 +12,7 @@
 SCOL = 2
 LANES = 128
 PAIRS = 4
-LOADS = 4
+LOADS = 2
 READY = 2304
 PARAMS = pltpu.CompilerParams(vmem_limit_bytes=16 * 1024 * 1024)
 MIDDLE = pltpu.CompilerParams(vmem_limit_bytes=24 * 1024 * 1024)
@@ -48,7 +48,7 @@
     return [cmul(low_c, low_s, high_c[:, b : b + 1], high_s[:, b : b + 1]) for b in range(blocks)]
 
 
-def first_axis_kernel(col_hbm, re_hbm, im_hbm, out_ref, col_ref, sky_ref, base_ref, step_ref, sem):
+def first_axis_kernel(col_hbm, re_hbm, im_hbm, out_ref, col_ref, sky_ref, base_ref, step_ref, acc_ref, sem):
     pixels = re_hbm.shape[0]
     blocks = pixels // LANES
     part = pixels // LOADS
@@ -79,9 +79,9 @@
             base_ref[q, 0, :, lanes] = middle[b][0]
             base_ref[q, 1, :, lanes] = middle[b][1]
 
-    def table_rows(q, first):
+    def table_rows(q, first, span):
         cols = []
-        for b in range(blocks):
+        for b in span:
             lanes = slice(b * LANES, (b + 1) * LANES)
             bc, bs = base_ref[q, 0, :, lanes], base_ref[q, 1, :, lanes]
             up_c, up_s, down_c, down_s = [], [], [], []
@@ -96,11 +96,19 @@
             cols.append(jnp.concatenate(up_c + up_s + down_c + down_s, axis=0).astype(bf16))
         return jnp.concatenate(cols, axis=1)
 
-    for copy in copies:
-        copy.wait()
-    for q in range(SCOL):
-        for first in range(1, 17, PAIRS):
-            product = jnp.dot(table_rows(q, first), sky_ref[...], preferred_element_type=f32)
+    groups = [(q, first) for q in range(SCOL) for first in range(1, 17, PAIRS)]
+    for i in range(LOADS):
+        copies[2 * i].wait()
+        copies[2 * i + 1].wait()
+        span = range(i * blocks // LOADS, (i + 1) * blocks // LOADS)
+        pixel_rows = slice(i * part, (i + 1) * part)
+        for at, (q, first) in enumerate(groups):
+            product = jnp.dot(table_rows(q, first, span), sky_ref[pixel_rows, :], preferred_element_type=f32)
+            if i > 0:
+                product = product + acc_ref[at]
+            if i < LOADS - 1:
+                acc_ref[at] = product
+                continue
             side = 8 * PAIRS
             for k in range(2):
                 c = product[2 * k * side : (2 * k + 1) * side]
@@ -127,6 +135,7 @@
             pltpu.VMEM((pixels, 2 * LANES), bf16),
             pltpu.VMEM((SCOL, 2, 8, pixels), f32),
             pltpu.VMEM((2, 24, pixels), f32),
+            pltpu.VMEM((32 // PAIRS, 32 * PAIRS, 2 * LANES), f32),
             pltpu.SemaphoreType.DMA((1 + 2 * LOADS,)),
         ],
         compiler_params=WIDE,

time: 67.8 us -> 67.5 us (level)
  no operation moved by 1% of the time
where the time goes in v5:
time: 67.5 us; the launch traced here: 67.2 us
  blocking collectives  40.1 us (59%)
  starting transfers between devices  10.4 us (15%)
  Pallas kernels  10 us (15%)
  waiting for transfers between devices  5.2 us (8%)
  local copies, waits for them, and re-layouts  0.74 us (1%)
  between operations  0.74 us (1%)
    all_to_all x2, blocking collectives, exchange(): return lax.all_to_all(x, axis, split_axis=0, concat_axis=0, tiled=True)  40.1 us
    all_to_all x1, starting transfers between devices, exchange(): return lax.all_to_all(x, axis, split_axis=0, concat_axis=0, tiled=True)  10.4 us
    all_to_all x1, waiting for transfers between devices, exchange(): return lax.all_to_all(x, axis, split_axis=0, concat_axis=0, tiled=True)  5.2 us
    pallas_call x1, Pallas kernels, first_axis(): pl.pallas_call(first_axis_kernel, in_specs=[HBM] * 3, out_specs=VMEM, out...  4.4 us
    pallas_call x1, Pallas kernels, weights(): pl.pallas_call(weights_kernel, in_specs=[SMEM, SMEM, VMEM, VMEM], out_spe...  1.7 us
    pallas_call x1, Pallas kernels, second_axis(): pl.pallas_call(second_axis_kernel, in_specs=[VMEM] * 4, out_specs=VMEM, o...  1.46 us
    pallas_call x1, Pallas kernels, second_table(): pl.pallas_call(second_table_kernel, in_specs=[SMEM, SMEM], out_specs=[VME...  1.43 us
  transfers between devices with their start and end apart: 1, of which 1 were waited for; matrix products, arithmetic and copies ran while one was open for 0% of the time, Pallas kernels for 5%

profile of v5, /device:TPU:1, one launch (start us, length us, event | category | flops | bytes accessed | tf_op | source)
XLA Modules:
  0.0 67.2 jit_solution(5872892138777896111)
XLA Ops:
  0.6 0.0 copy-start.4
  0.6 0.0 copy-start.3
  0.7 0.0 copy-start.1
  0.7 0.0 copy-start
  0.7 4.4 %first_axis.1 = bf16[32,32,128]{2,1,0:T(8,128)(2,1)} custom-call(s32[2]{0:T(128)} %col_hbm.1, bf16[4096,128]{1,0:T(8,128)(2,1)} %bitcast.15, bf16[4096,128]{1,0:T(8,128)(2,1)} %bitcast.16), custom_call_target="tpu_custom_call" | custom-call | tf_op jit(solution)/shard_map/first_axis/pallas_call | solution.py:128
  5.1 10.4 %all-to-all-start = ((bf16[32,32,128]{2,1,0:T(8,128)(2,1)}), bf16[32,32,128]{2,1,0:T(8,128)(2,1)S(1)}, u32[]{:S(2)}, u32[]{:S(2)}) async-start(bf16[32,32,128]{2,1,0:T(8,128)(2,1)} %first_axis.1), calls=%async_computation | async-start | bytes 524288 | tf_op jit(solution)/shard_map/all_to_all | solution.py:339
  15.5 0.0 copy-done.4
  15.5 0.1 copy.10.kernel_ref
  15.6 0.0 copy-done.3
  15.6 1.4 %second_table.1 = (bf16[2304,512]{1,0:T(8,128)(2,1)S(1)}, f32[2,48,256]{2,1,0:T(8,128)S(1)}, f32[4,16,128]{2,1,0:T(8,128)S(1)}) custom-call(s32[1]{0:T(128)} %bitcast.5.start_ref, s32[16]{0:T(128)S(1)} %copy-done.3), custom_call_target="tpu_custom_call" | custom-call | tf_op jit(solution)/shard_map/second_table/pallas_call | solution.py:192
  17.0 0.0 copy-done.1
  17.0 0.0 copy-done
  17.0 0.0 copy-start.2
  17.0 0.6 copy-done.2
  17.7 1.7 %weights.1 = (bf16[256,512]{1,0:T(8,128)(2,1)S(1)}, bf16[512,512]{1,0:T(8,128)(2,1)S(1)}) custom-call(s32[4]{0:T(128)S(1)} %bitcast.14, f32[16,8]{1,0:T(8,128)S(1)} %copy.10.kernel_ref, s32[2,4,128]{2,1,0:T(4,128)S(1)} %bitcast.12, s32[2,4,128]{2,1,0:T(4,128)S(1)} %bitcast.13), custom_call_target="tpu_custom_call" | custom-call | tf_op jit(solution)/shard_map/weights/pallas_call | solution.py:305
  19.4 5.2 %all-to-all-done.band_ref = bf16[32,32,128]{2,1,0:T(8,128)(2,1)S(1)} async-done(((bf16[32,32,128]{2,1,0:T(8,128)(2,1)}), bf16[32,32,128]{2,1,0:T(8,128)(2,1)S(1)}, u32[]{:S(2)}, u32[]{:S(2)}) %all-to-all-start) | async-done | bytes 262176 | tf_op jit(solution)/shard_map/all_to_all | solution.py:339
  24.6 1.5 %second_axis.1 = bf16[128,512]{1,0:T(8,128)(2,1)S(1)} custom-call(bf16[32,32,128]{2,1,0:T(8,128)(2,1)S(1)} %all-to-all-done.band_ref, bf16[2304,512]{1,0:T(8,128)(2,1)S(1)} %get-tuple-element.15.ready_ref, f32[2,48,256]{2,1,0:T(8,128)S(1)} %get-tuple-element.16.parts_ref, f32[4,16,128]{2,1,0:T(8,128)S(1)} %get-tuple-element.17.phases_ref), custom_call_target="tpu_custom_call" | custom-call | tf_op jit(solution)/shard_map/second_axis/pallas_call | solution.py:247
  26.1 24.9 %all_to_all.15.terms_ref = bf16[16,8,512]{2,1,0:T(8,128)(2,1)S(1)} all-to-all(bf16[16,8,512]{2,1,0:T(8,128)(2,1)S(1)} %bitcast.11), channel_id=1, replica_groups=mesh['facet'=16,'col'=32] {'facet'}, dimensions={0} | all-to-all | bytes 262144 | tf_op jit(solution)/shard_map/all_to_all | solution.py:339
  51.0 15.2 %all_to_all.16 = bf16[32,8,512]{2,1,0:T(8,128)(2,1)S(1)} all-to-all(bf16[32,8,512]{2,1,0:T(8,128)(2,1)S(1)} %own_rows.1), channel_id=1, replica_groups=mesh['facet'=16,'col'=32] {'col'}, dimensions={0} | all-to-all | bytes 524288 | tf_op jit(solution)/shard_map/all_to_all | solution.py:339
  66.2 1.0 %degrid.1 = (f32[4,128]{1,0:T(4,128)}, f32[4,128]{1,0:T(4,128)}) custom-call(bf16[256,512]{1,0:T(8,128)(2,1)S(1)} %bitcast.10, bf16[256,512]{1,0:T(8,128)(2,1)S(1)} %get-tuple-element.18.row_ref, bf16[512,512]{1,0:T(8,128)(2,1)S(1)} %get-tuple-element.19.col_ref), custom_call_target="tpu_custom_call" | custom-call | tf_op jit(solution)/shard_map/degrid/pallas_call | solution.py:328
  (1 shorter events, 0.0 us)
Async XLA Ops:
  0.6 14.9 %copy-start.4 = (f32[16,8]{0,1:T(8,128)S(1)}, f32[16,8]{0,1:T(8,128)}, u32[]{:S(2)}) copy-start(f32[16,8]{0,1:T(8,128)} %param.12) | copy-start | bytes 1540
  0.6 14.9 %copy-start.3 = (s32[16]{0:T(128)S(1)}, s32[16]{0:T(128)}, u32[]{:S(2)}) copy-start(s32[16]{0:T(128)} %sub_ref.1) | copy-start | bytes 196
  0.7 16.4 %copy-start.1 = (s32[2,1,4,128]{3,2,1,0:T(4,128)S(1)}, s32[2,1,4,128]{3,2,1,0:T(4,128)}, u32[]{:S(2)}) copy-start(s32[2,1,4,128]{3,2,1,0:T(4,128)} %param.15) | copy-start | bytes 12292
  0.7 16.4 %copy-start = (s32[2,1,4,128]{3,2,1,0:T(4,128)S(1)}, s32[2,1,4,128]{3,2,1,0:T(4,128)}, u32[]{:S(2)}) copy-start(s32[2,1,4,128]{3,2,1,0:T(4,128)} %param.14) | copy-start | bytes 12292
  5.1 19.5 %all-to-all-start = ((bf16[32,32,128]{2,1,0:T(8,128)(2,1)}), bf16[32,32,128]{2,1,0:T(8,128)(2,1)S(1)}, u32[]{:S(2)}, u32[]{:S(2)}) async-start(bf16[32,32,128]{2,1,0:T(8,128)(2,1)} %first_axis.1), calls=%async_computation | async-start | bytes 524288 | tf_op jit(solution)/shard_map/all_to_all | solution.py:339
  17.0 0.7 copy-start.2

commit v6 on v5

--- a/solution.py
+++ b/solution.py
@@ -12,8 +12,8 @@
 SCOL = 2
 LANES = 128
 PAIRS = 4
-LOADS = 2
-READY = 2304
+LOADS = 4
+READY = 2560
 PARAMS = pltpu.CompilerParams(vmem_limit_bytes=16 * 1024 * 1024)
 MIDDLE = pltpu.CompilerParams(vmem_limit_bytes=24 * 1024 * 1024)
 WIDE = pltpu.CompilerParams(vmem_limit_bytes=60 * 1024 * 1024)

time: 67.5 us -> 67.5 us (level)
  waiting for transfers between devices: 5.2 us -> 4.41 us
  local copies, waits for them, and re-layouts: 0.74 us -> 1.43 us
    all_to_all x1, waiting for transfers between devices: 5.2 us -> 4.41 us  [exchange(): return lax.all_to_all(x, axis, split_axis=0, concat_axis=0, tiled=True)]
    unnamed x11 -> x15, local copies, waits for them, and re-layouts: 0.74 us -> 1.43 us
where the time goes in v6:
time: 67.5 us; the launch traced here: 67.3 us
  blocking collectives  40.1 us (59%)
  starting transfers between devices  10.4 us (15%)
  Pallas kernels  10.2 us (15%)
  waiting for transfers between devices  4.41 us (7%)
  local copies, waits for them, and re-layouts  1.43 us (2%)
  between operations  0.75 us (1%)
    all_to_all x2, blocking collectives, exchange(): return lax.all_to_all(x, axis, split_axis=0, concat_axis=0, tiled=True)  40.1 us
    all_to_all x1, starting transfers between devices, exchange(): return lax.all_to_all(x, axis, split_axis=0, concat_axis=0, tiled=True)  10.4 us
    pallas_call x1, Pallas kernels, first_axis(): pl.pallas_call(first_axis_kernel, in_specs=[HBM] * 3, out_specs=VMEM, out...  4.45 us
    all_to_all x1, waiting for transfers between devices, exchange(): return lax.all_to_all(x, axis, split_axis=0, concat_axis=0, tiled=True)  4.41 us
    pallas_call x1, Pallas kernels, weights(): pl.pallas_call(weights_kernel, in_specs=[SMEM, SMEM, VMEM, VMEM], out_spe...  1.7 us
    pallas_call x1, Pallas kernels, second_table(): pl.pallas_call(second_table_kernel, in_specs=[SMEM, SMEM], out_specs=[VME...  1.52 us
    pallas_call x1, Pallas kernels, second_axis(): pl.pallas_call(second_axis_kernel, in_specs=[VMEM] * 4, out_specs=VMEM, o...  1.44 us
    unnamed x15, local copies, waits for them, and re-layouts  1.43 us
  transfers between devices with their start and end apart: 1, of which 1 were waited for; matrix products, arithmetic and copies ran while one was open for 0% of the time, Pallas kernels for 5%

profile of v6, /device:TPU:1, one launch (start us, length us, event | category | flops | bytes accessed | tf_op | source)
XLA Modules:
  0.0 67.3 jit_solution(7223743089022705733)
XLA Ops:
  0.6 0.0 copy-start.6
  0.6 0.0 copy-start.5
  0.7 0.0 copy-start.3
  0.7 0.0 copy-start.2
  0.7 4.5 %first_axis.1 = bf16[32,32,128]{2,1,0:T(8,128)(2,1)} custom-call(s32[2]{0:T(128)} %col_hbm.1, bf16[4096,128]{1,0:T(8,128)(2,1)} %bitcast.15, bf16[4096,128]{1,0:T(8,128)(2,1)} %bitcast.16), custom_call_target="tpu_custom_call" | custom-call | tf_op jit(solution)/shard_map/first_axis/pallas_call | solution.py:128
  5.1 10.4 %all-to-all-start = ((bf16[32,32,128]{2,1,0:T(8,128)(2,1)}), bf16[32,32,128]{2,1,0:T(8,128)(2,1)S(1)}, u32[]{:S(2)}, u32[]{:S(2)}) async-start(bf16[32,32,128]{2,1,0:T(8,128)(2,1)} %first_axis.1), calls=%async_computation | async-start | bytes 524288 | tf_op jit(solution)/shard_map/all_to_all | solution.py:339
  15.6 0.0 copy-done.6
  15.6 0.1 copy.10.kernel_ref
  15.6 0.0 copy-done.5
  15.6 1.5 %second_table.1 = (bf16[2560,512]{1,0:T(8,128)(2,1)S(1)}, f32[2,48,256]{2,1,0:T(8,128)S(1)}, f32[4,16,128]{2,1,0:T(8,128)S(1)}) custom-call(s32[1]{0:T(128)} %bitcast.5.start_ref, s32[16]{0:T(128)S(1)} %copy-done.5), custom_call_target="tpu_custom_call" | custom-call | tf_op jit(solution)/shard_map/second_table/pallas_call | solution.py:192
  17.2 0.0 copy-done.3
  17.2 0.0 copy-done.2
  17.2 0.0 copy-start.4
  17.2 0.6 copy-done.4
  17.8 1.7 %weights.1 = (bf16[256,512]{1,0:T(8,128)(2,1)S(1)}, bf16[512,512]{1,0:T(8,128)(2,1)S(1)}) custom-call(s32[4]{0:T(128)S(1)} %bitcast.14, f32[16,8]{1,0:T(8,128)S(1)} %copy.10.kernel_ref, s32[2,4,128]{2,1,0:T(4,128)S(1)} %bitcast.12, s32[2,4,128]{2,1,0:T(4,128)S(1)} %bitcast.13), custom_call_target="tpu_custom_call" | custom-call | tf_op jit(solution)/shard_map/weights/pallas_call | solution.py:305
  19.5 0.0 copy-start
  19.6 0.7 %copy-done = bf16[256,512]{1,0:T(8,128)(2,1)} copy-done((bf16[256,512]{1,0:T(8,128)(2,1)}, bf16[256,512]{1,0:T(8,128)(2,1)S(1)}, u32[]{:S(2)}) %copy-start) | copy-done | bytes 262168
  20.2 4.4 %all-to-all-done.band_ref = bf16[32,32,128]{2,1,0:T(8,128)(2,1)S(1)} async-done(((bf16[32,32,128]{2,1,0:T(8,128)(2,1)}), bf16[32,32,128]{2,1,0:T(8,128)(2,1)S(1)}, u32[]{:S(2)}, u32[]{:S(2)}) %all-to-all-start) | async-done | bytes 262176 | tf_op jit(solution)/shard_map/all_to_all | solution.py:339
  24.6 0.0 copy-start.1
  24.7 1.4 %second_axis.1 = bf16[128,512]{1,0:T(8,128)(2,1)S(1)} custom-call(bf16[32,32,128]{2,1,0:T(8,128)(2,1)S(1)} %all-to-all-done.band_ref, bf16[2560,512]{1,0:T(8,128)(2,1)S(1)} %get-tuple-element.15.ready_ref, f32[2,48,256]{2,1,0:T(8,128)S(1)} %get-tuple-element.16.parts_ref, f32[4,16,128]{2,1,0:T(8,128)S(1)} %get-tuple-element.17.phases_ref), custom_call_target="tpu_custom_call" | custom-call | tf_op jit(solution)/shard_map/second_axis/pallas_call | solution.py:247
  26.1 24.9 %all_to_all.15.terms_ref = bf16[16,8,512]{2,1,0:T(8,128)(2,1)S(1)} all-to-all(bf16[16,8,512]{2,1,0:T(8,128)(2,1)S(1)} %bitcast.11), channel_id=1, replica_groups=mesh['facet'=16,'col'=32] {'facet'}, dimensions={0} | all-to-all | bytes 262144 | tf_op jit(solution)/shard_map/all_to_all | solution.py:339
  51.1 15.2 %all_to_all.16 = bf16[32,8,512]{2,1,0:T(8,128)(2,1)S(1)} all-to-all(bf16[32,8,512]{2,1,0:T(8,128)(2,1)S(1)} %own_rows.1), channel_id=1, replica_groups=mesh['facet'=16,'col'=32] {'col'}, dimensions={0} | all-to-all | bytes 524288 | tf_op jit(solution)/shard_map/all_to_all | solution.py:339
  66.2 0.0 copy-done.1
  66.2 1.0 %degrid.1 = (f32[4,128]{1,0:T(4,128)}, f32[4,128]{1,0:T(4,128)}) custom-call(bf16[256,512]{1,0:T(8,128)(2,1)S(1)} %bitcast.10, bf16[256,512]{1,0:T(8,128)(2,1)S(1)} %copy-done.1, bf16[512,512]{1,0:T(8,128)(2,1)S(1)} %get-tuple-element.19.col_ref), custom_call_target="tpu_custom_call" | custom-call | tf_op jit(solution)/shard_map/degrid/pallas_call | solution.py:328
  (1 shorter events, 0.0 us)
Async XLA Ops:
  0.6 14.9 %copy-start.6 = (f32[16,8]{0,1:T(8,128)S(1)}, f32[16,8]{0,1:T(8,128)}, u32[]{:S(2)}) copy-start(f32[16,8]{0,1:T(8,128)} %param.12) | copy-start | bytes 1540
  0.6 15.0 %copy-start.5 = (s32[16]{0:T(128)S(1)}, s32[16]{0:T(128)}, u32[]{:S(2)}) copy-start(s32[16]{0:T(128)} %sub_ref.1) | copy-start | bytes 196
  0.7 16.5 %copy-start.3 = (s32[2,1,4,128]{3,2,1,0:T(4,128)S(1)}, s32[2,1,4,128]{3,2,1,0:T(4,128)}, u32[]{:S(2)}) copy-start(s32[2,1,4,128]{3,2,1,0:T(4,128)} %param.15) | copy-start | bytes 12292
  0.7 16.5 %copy-start.2 = (s32[2,1,4,128]{3,2,1,0:T(4,128)S(1)}, s32[2,1,4,128]{3,2,1,0:T(4,128)}, u32[]{:S(2)}) copy-start(s32[2,1,4,128]{3,2,1,0:T(4,128)} %param.14) | copy-start | bytes 12292
  5.1 19.5 %all-to-all-start = ((bf16[32,32,128]{2,1,0:T(8,128)(2,1)}), bf16[32,32,128]{2,1,0:T(8,128)(2,1)S(1)}, u32[]{:S(2)}, u32[]{:S(2)}) async-start(bf16[32,32,128]{2,1,0:T(8,128)(2,1)} %first_axis.1), calls=%async_computation | async-start | bytes 524288 | tf_op jit(solution)/shard_map/all_to_all | solution.py:339
  17.2 0.7 copy-start.4
  19.5 0.7 %copy-start = (bf16[256,512]{1,0:T(8,128)(2,1)}, bf16[256,512]{1,0:T(8,128)(2,1)S(1)}, u32[]{:S(2)}) copy-start(bf16[256,512]{1,0:T(8,128)(2,1)S(1)} %get-tuple-element.18.row_ref) | copy-start | bytes 786436
  24.6 41.6 %copy-start.1 = (bf16[256,512]{1,0:T(8,128)(2,1)S(1)}, bf16[256,512]{1,0:T(8,128)(2,1)}, u32[]{:S(2)}) copy-start(bf16[256,512]{1,0:T(8,128)(2,1)} %copy-done) | copy-start | bytes 786436

commit v7 on v5

--- a/solution.py
+++ b/solution.py
@@ -48,7 +48,7 @@
     return [cmul(low_c, low_s, high_c[:, b : b + 1], high_s[:, b : b + 1]) for b in range(blocks)]
 
 
-def first_axis_kernel(col_hbm, re_hbm, im_hbm, out_ref, col_ref, sky_ref, base_ref, step_ref, acc_ref, sem):
+def first_axis_kernel(col_hbm, re_hbm, im_hbm, out_hbm, col_ref, sky_ref, base_ref, step_ref, acc_ref, stage_ref, sem):
     pixels = re_hbm.shape[0]
     blocks = pixels // LANES
     part = pixels // LOADS
@@ -96,6 +96,7 @@
             cols.append(jnp.concatenate(up_c + up_s + down_c + down_s, axis=0).astype(bf16))
         return jnp.concatenate(cols, axis=1)
 
+    sent = []
     groups = [(q, first) for q in range(SCOL) for first in range(1, 17, PAIRS)]
     for i in range(LOADS):
         copies[2 * i].wait()
@@ -120,7 +121,14 @@
                     group = 16 - d if k == 1 else 16 if d == 16 else 16 + d
                     rows = slice(8 * t, 8 * t + 8)
                     both = jnp.concatenate([real[rows], imag[rows]], axis=0)
-                    out_ref[group, q * 16 : q * 16 + 16, :] = both.astype(bf16)
+                    stage_ref[group, q * 16 : q * 16 + 16, :] = both.astype(bf16)
+            if first + PAIRS > 16:
+                rows = pl.ds(q * 16, 16)
+                out_copy = pltpu.make_async_copy(stage_ref.at[:, rows], out_hbm.at[:, rows], sem.at[1 + 2 * LOADS + q])
+                out_copy.start()
+                sent.append(out_copy)
+    for copy in sent:
+        copy.wait()
 
 
 def first_axis(col_offsets, sky_re, sky_im):
@@ -128,7 +136,7 @@
     return pl.pallas_call(
         first_axis_kernel,
         in_specs=[HBM] * 3,
-        out_specs=VMEM,
+        out_specs=HBM,
         out_shape=jax.ShapeDtypeStruct((32, 32, LANES), bf16),
         scratch_shapes=[
             pltpu.SMEM((SCOL,), jnp.int32),
@@ -136,7 +144,8 @@
             pltpu.VMEM((SCOL, 2, 8, pixels), f32),
             pltpu.VMEM((2, 24, pixels), f32),
             pltpu.VMEM((32 // PAIRS, 32 * PAIRS, 2 * LANES), f32),
-            pltpu.SemaphoreType.DMA((1 + 2 * LOADS,)),
+            pltpu.VMEM((32, 32, LANES), bf16),
+            pltpu.SemaphoreType.DMA((1 + 2 * LOADS + SCOL,)),
         ],
         compiler_params=WIDE,
         name="first_axis",

time: 67.5 us -> 67.5 us (level)
  no operation moved by 1% of the time
where the time goes in v7:
time: 67.5 us; the launch traced here: 67.2 us
  blocking collectives  40.1 us (59%)
  starting transfers between devices  10.4 us (15%)
  Pallas kernels  10 us (15%)
  waiting for transfers between devices  5.2 us (8%)
  local copies, waits for them, and re-layouts  0.74 us (1%)
  between operations  0.74 us (1%)
    all_to_all x2, blocking collectives, exchange(): return lax.all_to_all(x, axis, split_axis=0, concat_axis=0, tiled=True)  40.1 us
    all_to_all x1, starting transfers between devices, exchange(): return lax.all_to_all(x, axis, split_axis=0, concat_axis=0, tiled=True)  10.4 us
    all_to_all x1, waiting for transfers between devices, exchange(): return lax.all_to_all(x, axis, split_axis=0, concat_axis=0, tiled=True)  5.2 us
    pallas_call x1, Pallas kernels, first_axis(): pl.pallas_call(first_axis_kernel, in_specs=[HBM] * 3, out_specs=HBM, out_...  4.36 us
    pallas_call x1, Pallas kernels, weights(): pl.pallas_call(weights_kernel, in_specs=[SMEM, SMEM, VMEM, VMEM], out_spe...  1.7 us
    pallas_call x1, Pallas kernels, second_axis(): pl.pallas_call(second_axis_kernel, in_specs=[VMEM] * 4, out_specs=VMEM, o...  1.47 us
    pallas_call x1, Pallas kernels, second_table(): pl.pallas_call(second_table_kernel, in_specs=[SMEM, SMEM], out_specs=[VME...  1.43 us
  transfers between devices with their start and end apart: 1, of which 1 were waited for; matrix products, arithmetic and copies ran while one was open for 0% of the time, Pallas kernels for 5%

profile of v7, /device:TPU:1, one launch (start us, length us, event | category | flops | bytes accessed | tf_op | source)
XLA Modules:
  0.0 67.2 jit_solution(9214928398645795766)
XLA Ops:
  0.6 0.0 copy-start.4
  0.6 0.0 copy-start.3
  0.7 0.0 copy-start.1
  0.7 0.0 copy-start
  0.7 4.4 %first_axis.1 = bf16[32,32,128]{2,1,0:T(8,128)(2,1)} custom-call(s32[2]{0:T(128)} %col_hbm.1, bf16[4096,128]{1,0:T(8,128)(2,1)} %bitcast.15, bf16[4096,128]{1,0:T(8,128)(2,1)} %bitcast.16), custom_call_target="tpu_custom_call" | custom-call | tf_op jit(solution)/shard_map/first_axis/pallas_call | solution.py:136
  5.0 10.4 %all-to-all-start = ((bf16[32,32,128]{2,1,0:T(8,128)(2,1)}), bf16[32,32,128]{2,1,0:T(8,128)(2,1)S(1)}, u32[]{:S(2)}, u32[]{:S(2)}) async-start(bf16[32,32,128]{2,1,0:T(8,128)(2,1)} %first_axis.1), calls=%async_computation | async-start | bytes 524288 | tf_op jit(solution)/shard_map/all_to_all | solution.py:348
  15.5 0.0 copy-done.4
  15.5 0.1 copy.10.kernel_ref
  15.5 0.0 copy-done.3
  15.5 1.4 %second_table.1 = (bf16[2304,512]{1,0:T(8,128)(2,1)S(1)}, f32[2,48,256]{2,1,0:T(8,128)S(1)}, f32[4,16,128]{2,1,0:T(8,128)S(1)}) custom-call(s32[1]{0:T(128)} %bitcast.5.start_ref, s32[16]{0:T(128)S(1)} %copy-done.3), custom_call_target="tpu_custom_call" | custom-call | tf_op jit(solution)/shard_map/second_table/pallas_call | solution.py:201
  17.0 0.0 copy-done.1
  17.0 0.0 copy-done
  17.0 0.0 copy-start.2
  17.0 0.6 copy-done.2
  17.7 1.7 %weights.1 = (bf16[256,512]{1,0:T(8,128)(2,1)S(1)}, bf16[512,512]{1,0:T(8,128)(2,1)S(1)}) custom-call(s32[4]{0:T(128)S(1)} %bitcast.14, f32[16,8]{1,0:T(8,128)S(1)} %copy.10.kernel_ref, s32[2,4,128]{2,1,0:T(4,128)S(1)} %bitcast.12, s32[2,4,128]{2,1,0:T(4,128)S(1)} %bitcast.13), custom_call_target="tpu_custom_call" | custom-call | tf_op jit(solution)/shard_map/weights/pallas_call | solution.py:314
  19.4 5.2 %all-to-all-done.band_ref = bf16[32,32,128]{2,1,0:T(8,128)(2,1)S(1)} async-done(((bf16[32,32,128]{2,1,0:T(8,128)(2,1)}), bf16[32,32,128]{2,1,0:T(8,128)(2,1)S(1)}, u32[]{:S(2)}, u32[]{:S(2)}) %all-to-all-start) | async-done | bytes 262176 | tf_op jit(solution)/shard_map/all_to_all | solution.py:348
  24.6 1.5 %second_axis.1 = bf16[128,512]{1,0:T(8,128)(2,1)S(1)} custom-call(bf16[32,32,128]{2,1,0:T(8,128)(2,1)S(1)} %all-to-all-done.band_ref, bf16[2304,512]{1,0:T(8,128)(2,1)S(1)} %get-tuple-element.15.ready_ref, f32[2,48,256]{2,1,0:T(8,128)S(1)} %get-tuple-element.16.parts_ref, f32[4,16,128]{2,1,0:T(8,128)S(1)} %get-tuple-element.17.phases_ref), custom_call_target="tpu_custom_call" | custom-call | tf_op jit(solution)/shard_map/second_axis/pallas_call | solution.py:256
  26.0 24.9 %all_to_all.15.terms_ref = bf16[16,8,512]{2,1,0:T(8,128)(2,1)S(1)} all-to-all(bf16[16,8,512]{2,1,0:T(8,128)(2,1)S(1)} %bitcast.11), channel_id=1, replica_groups=mesh['facet'=16,'col'=32] {'facet'}, dimensions={0} | all-to-all | bytes 262144 | tf_op jit(solution)/shard_map/all_to_all | solution.py:348
  51.0 15.1 %all_to_all.16 = bf16[32,8,512]{2,1,0:T(8,128)(2,1)S(1)} all-to-all(bf16[32,8,512]{2,1,0:T(8,128)(2,1)S(1)} %own_rows.1), channel_id=1, replica_groups=mesh['facet'=16,'col'=32] {'col'}, dimensions={0} | all-to-all | bytes 524288 | tf_op jit(solution)/shard_map/all_to_all | solution.py:348
  66.2 1.0 %degrid.1 = (f32[4,128]{1,0:T(4,128)}, f32[4,128]{1,0:T(4,128)}) custom-call(bf16[256,512]{1,0:T(8,128)(2,1)S(1)} %bitcast.10, bf16[256,512]{1,0:T(8,128)(2,1)S(1)} %get-tuple-element.18.row_ref, bf16[512,512]{1,0:T(8,128)(2,1)S(1)} %get-tuple-element.19.col_ref), custom_call_target="tpu_custom_call" | custom-call | tf_op jit(solution)/shard_map/degrid/pallas_call | solution.py:337
  (1 shorter events, 0.0 us)
Async XLA Ops:
  0.6 14.8 %copy-start.4 = (f32[16,8]{0,1:T(8,128)S(1)}, f32[16,8]{0,1:T(8,128)}, u32[]{:S(2)}) copy-start(f32[16,8]{0,1:T(8,128)} %param.12) | copy-start | bytes 1540
  0.6 14.9 %copy-start.3 = (s32[16]{0:T(128)S(1)}, s32[16]{0:T(128)}, u32[]{:S(2)}) copy-start(s32[16]{0:T(128)} %sub_ref.1) | copy-start | bytes 196
  0.7 16.3 %copy-start.1 = (s32[2,1,4,128]{3,2,1,0:T(4,128)S(1)}, s32[2,1,4,128]{3,2,1,0:T(4,128)}, u32[]{:S(2)}) copy-start(s32[2,1,4,128]{3,2,1,0:T(4,128)} %param.15) | copy-start | bytes 12292
  0.7 16.3 %copy-start = (s32[2,1,4,128]{3,2,1,0:T(4,128)S(1)}, s32[2,1,4,128]{3,2,1,0:T(4,128)}, u32[]{:S(2)}) copy-start(s32[2,1,4,128]{3,2,1,0:T(4,128)} %param.14) | copy-start | bytes 12292
  5.0 19.5 %all-to-all-start = ((bf16[32,32,128]{2,1,0:T(8,128)(2,1)}), bf16[32,32,128]{2,1,0:T(8,128)(2,1)S(1)}, u32[]{:S(2)}, u32[]{:S(2)}) async-start(bf16[32,32,128]{2,1,0:T(8,128)(2,1)} %first_axis.1), calls=%async_computation | async-start | bytes 524288 | tf_op jit(solution)/shard_map/all_to_all | solution.py:348
  17.0 0.7 copy-start.2
